TPU v7x, 256 devices: a whole 4x4x8 slice. The times are simulated.
256 devices in a mesh: tm: 32 (over z, x), space: 8 (over y, core).
Axes of the slice: x: 4, y: 4, z: 8, core: 2. Of those that a mesh axis runs over, the one named last changes fastest.
Arguments:
- initial: float32 [64, 2048], P('space'), may hold values from -6 to 6
- source: float32 [64, 2048], P('space'), may hold values from -3 to 3
- diff_rate: float32 [64, 2048], P('space'), may hold values from 0.004 to 0.04
- vel_x: float32 [64, 2048], P('space'), may hold values from -0.04 to 0.04
- vel_y: float32 [64, 2048], P('space'), may hold values from -0.04 to 0.04
- amp: float32 [256], P('tm'), may hold values from 0.5 to 1.5
- c_guess: float32 [64, 64, 2048], P('tm', 'space'), may hold values from -6 to 6
Outputs:
- corrected: float32 [64, 64, 2048], P('tm', 'space')
All inputs are finite; a program needn't handle non-finite values.
Results may differ from a plain program's by a relative error of at most 0.00002.
Values sent between devices are 32-bit elements; how exact they have to be, the bound alone decides.
A program may use at most 64 MiB of HBM per device.

v0:
```python
import jax
import jax.numpy as jnp
from jax import lax
from jax.sharding import PartitionSpec as P

M = 4


def padded_2(block, sides, width):
    for axis, dim in sides:
        count = lax.axis_size(axis)
        forward = [(i, i + 1) for i in range(count - 1)]
        backward = [(target, source) for source, target in forward]
        low = lax.ppermute(
            lax.slice_in_dim(block, block.shape[dim] - width, None, axis=dim), axis, forward
        )
        high = lax.ppermute(lax.slice_in_dim(block, 0, width, axis=dim), axis, backward)
        block = jnp.concatenate([low, block, high], axis=dim)
    return block


def shifted(value, axis, steps):
    count = lax.axis_size(axis)
    initial, last = (max(0, -steps), min(count, count - steps))
    return lax.ppermute(value, axis, [(source, source + steps) for source in range(initial, last)])


def advance(field, rate, along_x, along_y):
    rimmed = padded_2(field, (("space", 1),), 1)
    padded = jnp.pad(rimmed, ((0, 0), (0, 0), (1, 1)))
    row_up = padded[:, 2:, 1:-1]
    row_down = padded[:, :-2, 1:-1]
    col_up = padded[:, 1:-1, 2:]
    col_down = padded[:, 1:-1, :-2]
    spread = rate * (row_up + row_down + col_up + col_down - 4.0 * field)
    drift_x = jnp.maximum(along_x, 0.0) * (field - row_down) + jnp.minimum(along_x, 0.0) * (
        row_up - field
    )
    drift_y = jnp.maximum(along_y, 0.0) * (field - col_down) + jnp.minimum(along_y, 0.0) * (
        col_up - field
    )
    return field + spread - drift_x - drift_y


def per_device(initial, source, diff_rate, vel_x, vel_y, amp, c_guess):
    c_points = c_guess.shape[0]
    devices_time = lax.axis_size("tm")
    is_first = lax.axis_index("tm") == 0
    amps = amp.reshape(c_points, M)

    def propagate(starts):
        state = starts
        for step_index in range(M):
            state = (
                advance(state, diff_rate, vel_x, vel_y)
                + amps[:, step_index][:, None, None] * source[None]
            )
        return state

    def incoming(last_state):
        arrived = shifted(last_state, "tm", 1)
        return jnp.where(is_first, initial, arrived)

    starts_first = jnp.concatenate([incoming(c_guess[-1])[None], c_guess[:-1]], axis=0)
    relaxed = propagate(starts_first)
    starts_second = jnp.concatenate([incoming(relaxed[-1])[None], relaxed[:-1]], axis=0)
    resid = propagate(starts_second) - relaxed
    coarse_rate = M * diff_rate
    coarse_x = M * vel_x
    coarse_y = M * vel_y

    def coarse_step(error):
        return advance(error[None], coarse_rate, coarse_x, coarse_y)[0]

    def coarse_power(error, count):
        return lax.fori_loop(0, count, lambda step_index, value: coarse_step(value), error)

    def chain(entry):

        def chain_body(error, term):
            error = coarse_step(error) + term
            return (error, error)

        _, errors = lax.scan(chain_body, entry, resid)
        return errors

    zero_field = jnp.zeros(initial.shape, jnp.float32)
    local_last = chain(zero_field)[-1]

    def relay_round(round_index, carried):
        return shifted(coarse_power(carried, c_points) + local_last, "tm", 1)

    entry = lax.fori_loop(0, devices_time - 1, relay_round, zero_field)
    return relaxed + chain(entry)


def solution(mesh):
    in_specs = (
        P("space", None),
        P("space", None),
        P("space", None),
        P("space", None),
        P("space", None),
        P("tm"),
        P("tm", "space", None),
    )
    out_specs = P("tm", "space", None)
    return jax.shard_map(
        per_device, mesh=mesh, in_specs=in_specs, out_specs=out_specs, check_vma=False
    )
```

profile of v0, /device:TPU:144, one launch (start us, length us, event | category | flops | bytes accessed | tf_op | source)
XLA Modules:
  0.0 852.4 jit_solution(8326470758702305589)
XLA Ops:
  93.8 743.0 %while.61 = (s32[]{:T(128)}, f32[8,2048]{1,0:T(8,128)S(1)}, f32[8,2048]{1,0:T(8,128)S(1)}, f32[8,2048]{1,0:T(8,128)S(1)}, f32[8,2048]{1,0:T(8,128)S(1)}, /*index...) while((s32[]{:T(128)}, f32[8,2048]{1,0:T(8,128)S(1)}, f32[8,2048]{1,0:T(8,128)S(1)}, ...), condition=%wide.region_5.6_spmd, body=%wide.region_2.5_spmd.sunk | while | flops 589988 | bytes 1393058 | solution.py:93
  93.8 14.4 %while.63 = (s32[]{:T(128)}, f32[8,2048]{1,0:T(8,128)S(1)}, f32[8,2048]{1,0:T(8,128)S(1)}, f32[8,2048]{1,0:T(8,128)S(1)}, f32[8,2048]{1,0:T(8,128)S(1)}, /*index=5*/s32[]{:T(128)}) while((s32[]{:T(128)}, f32[8,2048]{1,0:T(8,128)S(1)}, f32[8,2048]{1,0:T(8,128)S(1)}, f32[8,2048]{1,0:T(8,128)S(1)}, f32[8,2048]{1,0:T(8,128)S(1)}, ...), condition=%wide.region_4.4_spmd, body=%wide.region_3.3_spmd.sunk | while | flops 573602 | bytes 934117 | solution.py:76
  118.2 14.4 %while.63 = (s32[]{:T(128)}, f32[8,2048]{1,0:T(8,128)S(1)}, f32[8,2048]{1,0:T(8,128)S(1)}, f32[8,2048]{1,0:T(8,128)S(1)}, f32[8,2048]{1,0:T(8,128)S(1)}, /*index=5*/s32[]{:T(128)}) while((s32[]{:T(128)}, f32[8,2048]{1,0:T(8,128)S(1)}, f32[8,2048]{1,0:T(8,128)S(1)}, f32[8,2048]{1,0:T(8,128)S(1)}, f32[8,2048]{1,0:T(8,128)S(1)}, ...), condition=%wide.region_4.4_spmd, body=%wide.region_3.3_spmd.sunk | while | flops 573602 | bytes 934117 | solution.py:76
  142.8 14.4 %while.63 = (s32[]{:T(128)}, f32[8,2048]{1,0:T(8,128)S(1)}, f32[8,2048]{1,0:T(8,128)S(1)}, f32[8,2048]{1,0:T(8,128)S(1)}, f32[8,2048]{1,0:T(8,128)S(1)}, /*index=5*/s32[]{:T(128)}) while((s32[]{:T(128)}, f32[8,2048]{1,0:T(8,128)S(1)}, f32[8,2048]{1,0:T(8,128)S(1)}, f32[8,2048]{1,0:T(8,128)S(1)}, f32[8,2048]{1,0:T(8,128)S(1)}, ...), condition=%wide.region_4.4_spmd, body=%wide.region_3.3_spmd.sunk | while | flops 573602 | bytes 934117 | solution.py:76
  166.7 14.4 %while.63 = (s32[]{:T(128)}, f32[8,2048]{1,0:T(8,128)S(1)}, f32[8,2048]{1,0:T(8,128)S(1)}, f32[8,2048]{1,0:T(8,128)S(1)}, f32[8,2048]{1,0:T(8,128)S(1)}, /*index=5*/s32[]{:T(128)}) while((s32[]{:T(128)}, f32[8,2048]{1,0:T(8,128)S(1)}, f32[8,2048]{1,0:T(8,128)S(1)}, f32[8,2048]{1,0:T(8,128)S(1)}, f32[8,2048]{1,0:T(8,128)S(1)}, ...), condition=%wide.region_4.4_spmd, body=%wide.region_3.3_spmd.sunk | while | flops 573602 | bytes 934117 | solution.py:76
  190.7 14.4 %while.63 = (s32[]{:T(128)}, f32[8,2048]{1,0:T(8,128)S(1)}, f32[8,2048]{1,0:T(8,128)S(1)}, f32[8,2048]{1,0:T(8,128)S(1)}, f32[8,2048]{1,0:T(8,128)S(1)}, /*index=5*/s32[]{:T(128)}) while((s32[]{:T(128)}, f32[8,2048]{1,0:T(8,128)S(1)}, f32[8,2048]{1,0:T(8,128)S(1)}, f32[8,2048]{1,0:T(8,128)S(1)}, f32[8,2048]{1,0:T(8,128)S(1)}, ...), condition=%wide.region_4.4_spmd, body=%wide.region_3.3_spmd.sunk | while | flops 573602 | bytes 934117 | solution.py:76
  214.6 14.4 %while.63 = (s32[]{:T(128)}, f32[8,2048]{1,0:T(8,128)S(1)}, f32[8,2048]{1,0:T(8,128)S(1)}, f32[8,2048]{1,0:T(8,128)S(1)}, f32[8,2048]{1,0:T(8,128)S(1)}, /*index=5*/s32[]{:T(128)}) while((s32[]{:T(128)}, f32[8,2048]{1,0:T(8,128)S(1)}, f32[8,2048]{1,0:T(8,128)S(1)}, f32[8,2048]{1,0:T(8,128)S(1)}, f32[8,2048]{1,0:T(8,128)S(1)}, ...), condition=%wide.region_4.4_spmd, body=%wide.region_3.3_spmd.sunk | while | flops 573602 | bytes 934117 | solution.py:76
  238.5 14.4 %while.63 = (s32[]{:T(128)}, f32[8,2048]{1,0:T(8,128)S(1)}, f32[8,2048]{1,0:T(8,128)S(1)}, f32[8,2048]{1,0:T(8,128)S(1)}, f32[8,2048]{1,0:T(8,128)S(1)}, /*index=5*/s32[]{:T(128)}) while((s32[]{:T(128)}, f32[8,2048]{1,0:T(8,128)S(1)}, f32[8,2048]{1,0:T(8,128)S(1)}, f32[8,2048]{1,0:T(8,128)S(1)}, f32[8,2048]{1,0:T(8,128)S(1)}, ...), condition=%wide.region_4.4_spmd, body=%wide.region_3.3_spmd.sunk | while | flops 573602 | bytes 934117 | solution.py:76
  262.4 14.4 %while.63 = (s32[]{:T(128)}, f32[8,2048]{1,0:T(8,128)S(1)}, f32[8,2048]{1,0:T(8,128)S(1)}, f32[8,2048]{1,0:T(8,128)S(1)}, f32[8,2048]{1,0:T(8,128)S(1)}, /*index=5*/s32[]{:T(128)}) while((s32[]{:T(128)}, f32[8,2048]{1,0:T(8,128)S(1)}, f32[8,2048]{1,0:T(8,128)S(1)}, f32[8,2048]{1,0:T(8,128)S(1)}, f32[8,2048]{1,0:T(8,128)S(1)}, ...), condition=%wide.region_4.4_spmd, body=%wide.region_3.3_spmd.sunk | while | flops 573602 | bytes 934117 | solution.py:76
  286.4 14.4 %while.63 = (s32[]{:T(128)}, f32[8,2048]{1,0:T(8,128)S(1)}, f32[8,2048]{1,0:T(8,128)S(1)}, f32[8,2048]{1,0:T(8,128)S(1)}, f32[8,2048]{1,0:T(8,128)S(1)}, /*index=5*/s32[]{:T(128)}) while((s32[]{:T(128)}, f32[8,2048]{1,0:T(8,128)S(1)}, f32[8,2048]{1,0:T(8,128)S(1)}, f32[8,2048]{1,0:T(8,128)S(1)}, f32[8,2048]{1,0:T(8,128)S(1)}, ...), condition=%wide.region_4.4_spmd, body=%wide.region_3.3_spmd.sunk | while | flops 573602 | bytes 934117 | solution.py:76
  310.3 14.4 %while.63 = (s32[]{:T(128)}, f32[8,2048]{1,0:T(8,128)S(1)}, f32[8,2048]{1,0:T(8,128)S(1)}, f32[8,2048]{1,0:T(8,128)S(1)}, f32[8,2048]{1,0:T(8,128)S(1)}, /*index=5*/s32[]{:T(128)}) while((s32[]{:T(128)}, f32[8,2048]{1,0:T(8,128)S(1)}, f32[8,2048]{1,0:T(8,128)S(1)}, f32[8,2048]{1,0:T(8,128)S(1)}, f32[8,2048]{1,0:T(8,128)S(1)}, ...), condition=%wide.region_4.4_spmd, body=%wide.region_3.3_spmd.sunk | while | flops 573602 | bytes 934117 | solution.py:76
  334.2 14.4 %while.63 = (s32[]{:T(128)}, f32[8,2048]{1,0:T(8,128)S(1)}, f32[8,2048]{1,0:T(8,128)S(1)}, f32[8,2048]{1,0:T(8,128)S(1)}, f32[8,2048]{1,0:T(8,128)S(1)}, /*index=5*/s32[]{:T(128)}) while((s32[]{:T(128)}, f32[8,2048]{1,0:T(8,128)S(1)}, f32[8,2048]{1,0:T(8,128)S(1)}, f32[8,2048]{1,0:T(8,128)S(1)}, f32[8,2048]{1,0:T(8,128)S(1)}, ...), condition=%wide.region_4.4_spmd, body=%wide.region_3.3_spmd.sunk | while | flops 573602 | bytes 934117 | solution.py:76
  358.2 14.4 %while.63 = (s32[]{:T(128)}, f32[8,2048]{1,0:T(8,128)S(1)}, f32[8,2048]{1,0:T(8,128)S(1)}, f32[8,2048]{1,0:T(8,128)S(1)}, f32[8,2048]{1,0:T(8,128)S(1)}, /*index=5*/s32[]{:T(128)}) while((s32[]{:T(128)}, f32[8,2048]{1,0:T(8,128)S(1)}, f32[8,2048]{1,0:T(8,128)S(1)}, f32[8,2048]{1,0:T(8,128)S(1)}, f32[8,2048]{1,0:T(8,128)S(1)}, ...), condition=%wide.region_4.4_spmd, body=%wide.region_3.3_spmd.sunk | while | flops 573602 | bytes 934117 | solution.py:76
  382.1 14.4 %while.63 = (s32[]{:T(128)}, f32[8,2048]{1,0:T(8,128)S(1)}, f32[8,2048]{1,0:T(8,128)S(1)}, f32[8,2048]{1,0:T(8,128)S(1)}, f32[8,2048]{1,0:T(8,128)S(1)}, /*index=5*/s32[]{:T(128)}) while((s32[]{:T(128)}, f32[8,2048]{1,0:T(8,128)S(1)}, f32[8,2048]{1,0:T(8,128)S(1)}, f32[8,2048]{1,0:T(8,128)S(1)}, f32[8,2048]{1,0:T(8,128)S(1)}, ...), condition=%wide.region_4.4_spmd, body=%wide.region_3.3_spmd.sunk | while | flops 573602 | bytes 934117 | solution.py:76
  406.0 14.4 %while.63 = (s32[]{:T(128)}, f32[8,2048]{1,0:T(8,128)S(1)}, f32[8,2048]{1,0:T(8,128)S(1)}, f32[8,2048]{1,0:T(8,128)S(1)}, f32[8,2048]{1,0:T(8,128)S(1)}, /*index=5*/s32[]{:T(128)}) while((s32[]{:T(128)}, f32[8,2048]{1,0:T(8,128)S(1)}, f32[8,2048]{1,0:T(8,128)S(1)}, f32[8,2048]{1,0:T(8,128)S(1)}, f32[8,2048]{1,0:T(8,128)S(1)}, ...), condition=%wide.region_4.4_spmd, body=%wide.region_3.3_spmd.sunk | while | flops 573602 | bytes 934117 | solution.py:76
  430.0 14.4 %while.63 = (s32[]{:T(128)}, f32[8,2048]{1,0:T(8,128)S(1)}, f32[8,2048]{1,0:T(8,128)S(1)}, f32[8,2048]{1,0:T(8,128)S(1)}, f32[8,2048]{1,0:T(8,128)S(1)}, /*index=5*/s32[]{:T(128)}) while((s32[]{:T(128)}, f32[8,2048]{1,0:T(8,128)S(1)}, f32[8,2048]{1,0:T(8,128)S(1)}, f32[8,2048]{1,0:T(8,128)S(1)}, f32[8,2048]{1,0:T(8,128)S(1)}, ...), condition=%wide.region_4.4_spmd, body=%wide.region_3.3_spmd.sunk | while | flops 573602 | bytes 934117 | solution.py:76
  453.9 14.4 %while.63 = (s32[]{:T(128)}, f32[8,2048]{1,0:T(8,128)S(1)}, f32[8,2048]{1,0:T(8,128)S(1)}, f32[8,2048]{1,0:T(8,128)S(1)}, f32[8,2048]{1,0:T(8,128)S(1)}, /*index=5*/s32[]{:T(128)}) while((s32[]{:T(128)}, f32[8,2048]{1,0:T(8,128)S(1)}, f32[8,2048]{1,0:T(8,128)S(1)}, f32[8,2048]{1,0:T(8,128)S(1)}, f32[8,2048]{1,0:T(8,128)S(1)}, ...), condition=%wide.region_4.4_spmd, body=%wide.region_3.3_spmd.sunk | while | flops 573602 | bytes 934117 | solution.py:76
  477.8 14.4 %while.63 = (s32[]{:T(128)}, f32[8,2048]{1,0:T(8,128)S(1)}, f32[8,2048]{1,0:T(8,128)S(1)}, f32[8,2048]{1,0:T(8,128)S(1)}, f32[8,2048]{1,0:T(8,128)S(1)}, /*index=5*/s32[]{:T(128)}) while((s32[]{:T(128)}, f32[8,2048]{1,0:T(8,128)S(1)}, f32[8,2048]{1,0:T(8,128)S(1)}, f32[8,2048]{1,0:T(8,128)S(1)}, f32[8,2048]{1,0:T(8,128)S(1)}, ...), condition=%wide.region_4.4_spmd, body=%wide.region_3.3_spmd.sunk | while | flops 573602 | bytes 934117 | solution.py:76
  501.7 14.4 %while.63 = (s32[]{:T(128)}, f32[8,2048]{1,0:T(8,128)S(1)}, f32[8,2048]{1,0:T(8,128)S(1)}, f32[8,2048]{1,0:T(8,128)S(1)}, f32[8,2048]{1,0:T(8,128)S(1)}, /*index=5*/s32[]{:T(128)}) while((s32[]{:T(128)}, f32[8,2048]{1,0:T(8,128)S(1)}, f32[8,2048]{1,0:T(8,128)S(1)}, f32[8,2048]{1,0:T(8,128)S(1)}, f32[8,2048]{1,0:T(8,128)S(1)}, ...), condition=%wide.region_4.4_spmd, body=%wide.region_3.3_spmd.sunk | while | flops 573602 | bytes 934117 | solution.py:76
  525.7 14.4 %while.63 = (s32[]{:T(128)}, f32[8,2048]{1,0:T(8,128)S(1)}, f32[8,2048]{1,0:T(8,128)S(1)}, f32[8,2048]{1,0:T(8,128)S(1)}, f32[8,2048]{1,0:T(8,128)S(1)}, /*index=5*/s32[]{:T(128)}) while((s32[]{:T(128)}, f32[8,2048]{1,0:T(8,128)S(1)}, f32[8,2048]{1,0:T(8,128)S(1)}, f32[8,2048]{1,0:T(8,128)S(1)}, f32[8,2048]{1,0:T(8,128)S(1)}, ...), condition=%wide.region_4.4_spmd, body=%wide.region_3.3_spmd.sunk | while | flops 573602 | bytes 934117 | solution.py:76
  549.6 14.4 %while.63 = (s32[]{:T(128)}, f32[8,2048]{1,0:T(8,128)S(1)}, f32[8,2048]{1,0:T(8,128)S(1)}, f32[8,2048]{1,0:T(8,128)S(1)}, f32[8,2048]{1,0:T(8,128)S(1)}, /*index=5*/s32[]{:T(128)}) while((s32[]{:T(128)}, f32[8,2048]{1,0:T(8,128)S(1)}, f32[8,2048]{1,0:T(8,128)S(1)}, f32[8,2048]{1,0:T(8,128)S(1)}, f32[8,2048]{1,0:T(8,128)S(1)}, ...), condition=%wide.region_4.4_spmd, body=%wide.region_3.3_spmd.sunk | while | flops 573602 | bytes 934117 | solution.py:76
  573.5 14.4 %while.63 = (s32[]{:T(128)}, f32[8,2048]{1,0:T(8,128)S(1)}, f32[8,2048]{1,0:T(8,128)S(1)}, f32[8,2048]{1,0:T(8,128)S(1)}, f32[8,2048]{1,0:T(8,128)S(1)}, /*index=5*/s32[]{:T(128)}) while((s32[]{:T(128)}, f32[8,2048]{1,0:T(8,128)S(1)}, f32[8,2048]{1,0:T(8,128)S(1)}, f32[8,2048]{1,0:T(8,128)S(1)}, f32[8,2048]{1,0:T(8,128)S(1)}, ...), condition=%wide.region_4.4_spmd, body=%wide.region_3.3_spmd.sunk | while | flops 573602 | bytes 934117 | solution.py:76
  597.5 14.4 %while.63 = (s32[]{:T(128)}, f32[8,2048]{1,0:T(8,128)S(1)}, f32[8,2048]{1,0:T(8,128)S(1)}, f32[8,2048]{1,0:T(8,128)S(1)}, f32[8,2048]{1,0:T(8,128)S(1)}, /*index=5*/s32[]{:T(128)}) while((s32[]{:T(128)}, f32[8,2048]{1,0:T(8,128)S(1)}, f32[8,2048]{1,0:T(8,128)S(1)}, f32[8,2048]{1,0:T(8,128)S(1)}, f32[8,2048]{1,0:T(8,128)S(1)}, ...), condition=%wide.region_4.4_spmd, body=%wide.region_3.3_spmd.sunk | while | flops 573602 | bytes 934117 | solution.py:76
  621.4 14.4 %while.63 = (s32[]{:T(128)}, f32[8,2048]{1,0:T(8,128)S(1)}, f32[8,2048]{1,0:T(8,128)S(1)}, f32[8,2048]{1,0:T(8,128)S(1)}, f32[8,2048]{1,0:T(8,128)S(1)}, /*index=5*/s32[]{:T(128)}) while((s32[]{:T(128)}, f32[8,2048]{1,0:T(8,128)S(1)}, f32[8,2048]{1,0:T(8,128)S(1)}, f32[8,2048]{1,0:T(8,128)S(1)}, f32[8,2048]{1,0:T(8,128)S(1)}, ...), condition=%wide.region_4.4_spmd, body=%wide.region_3.3_spmd.sunk | while | flops 573602 | bytes 934117 | solution.py:76
  645.3 14.4 %while.63 = (s32[]{:T(128)}, f32[8,2048]{1,0:T(8,128)S(1)}, f32[8,2048]{1,0:T(8,128)S(1)}, f32[8,2048]{1,0:T(8,128)S(1)}, f32[8,2048]{1,0:T(8,128)S(1)}, /*index=5*/s32[]{:T(128)}) while((s32[]{:T(128)}, f32[8,2048]{1,0:T(8,128)S(1)}, f32[8,2048]{1,0:T(8,128)S(1)}, f32[8,2048]{1,0:T(8,128)S(1)}, f32[8,2048]{1,0:T(8,128)S(1)}, ...), condition=%wide.region_4.4_spmd, body=%wide.region_3.3_spmd.sunk | while | flops 573602 | bytes 934117 | solution.py:76
  669.3 14.4 %while.63 = (s32[]{:T(128)}, f32[8,2048]{1,0:T(8,128)S(1)}, f32[8,2048]{1,0:T(8,128)S(1)}, f32[8,2048]{1,0:T(8,128)S(1)}, f32[8,2048]{1,0:T(8,128)S(1)}, /*index=5*/s32[]{:T(128)}) while((s32[]{:T(128)}, f32[8,2048]{1,0:T(8,128)S(1)}, f32[8,2048]{1,0:T(8,128)S(1)}, f32[8,2048]{1,0:T(8,128)S(1)}, f32[8,2048]{1,0:T(8,128)S(1)}, ...), condition=%wide.region_4.4_spmd, body=%wide.region_3.3_spmd.sunk | while | flops 573602 | bytes 934117 | solution.py:76
  693.2 14.4 %while.63 = (s32[]{:T(128)}, f32[8,2048]{1,0:T(8,128)S(1)}, f32[8,2048]{1,0:T(8,128)S(1)}, f32[8,2048]{1,0:T(8,128)S(1)}, f32[8,2048]{1,0:T(8,128)S(1)}, /*index=5*/s32[]{:T(128)}) while((s32[]{:T(128)}, f32[8,2048]{1,0:T(8,128)S(1)}, f32[8,2048]{1,0:T(8,128)S(1)}, f32[8,2048]{1,0:T(8,128)S(1)}, f32[8,2048]{1,0:T(8,128)S(1)}, ...), condition=%wide.region_4.4_spmd, body=%wide.region_3.3_spmd.sunk | while | flops 573602 | bytes 934117 | solution.py:76
  717.1 14.4 %while.63 = (s32[]{:T(128)}, f32[8,2048]{1,0:T(8,128)S(1)}, f32[8,2048]{1,0:T(8,128)S(1)}, f32[8,2048]{1,0:T(8,128)S(1)}, f32[8,2048]{1,0:T(8,128)S(1)}, /*index=5*/s32[]{:T(128)}) while((s32[]{:T(128)}, f32[8,2048]{1,0:T(8,128)S(1)}, f32[8,2048]{1,0:T(8,128)S(1)}, f32[8,2048]{1,0:T(8,128)S(1)}, f32[8,2048]{1,0:T(8,128)S(1)}, ...), condition=%wide.region_4.4_spmd, body=%wide.region_3.3_spmd.sunk | while | flops 573602 | bytes 934117 | solution.py:76
  741.0 14.4 %while.63 = (s32[]{:T(128)}, f32[8,2048]{1,0:T(8,128)S(1)}, f32[8,2048]{1,0:T(8,128)S(1)}, f32[8,2048]{1,0:T(8,128)S(1)}, f32[8,2048]{1,0:T(8,128)S(1)}, /*index=5*/s32[]{:T(128)}) while((s32[]{:T(128)}, f32[8,2048]{1,0:T(8,128)S(1)}, f32[8,2048]{1,0:T(8,128)S(1)}, f32[8,2048]{1,0:T(8,128)S(1)}, f32[8,2048]{1,0:T(8,128)S(1)}, ...), condition=%wide.region_4.4_spmd, body=%wide.region_3.3_spmd.sunk | while | flops 573602 | bytes 934117 | solution.py:76
  765.0 14.4 %while.63 = (s32[]{:T(128)}, f32[8,2048]{1,0:T(8,128)S(1)}, f32[8,2048]{1,0:T(8,128)S(1)}, f32[8,2048]{1,0:T(8,128)S(1)}, f32[8,2048]{1,0:T(8,128)S(1)}, /*index=5*/s32[]{:T(128)}) while((s32[]{:T(128)}, f32[8,2048]{1,0:T(8,128)S(1)}, f32[8,2048]{1,0:T(8,128)S(1)}, f32[8,2048]{1,0:T(8,128)S(1)}, f32[8,2048]{1,0:T(8,128)S(1)}, ...), condition=%wide.region_4.4_spmd, body=%wide.region_3.3_spmd.sunk | while | flops 573602 | bytes 934117 | solution.py:76
  788.9 14.4 %while.63 = (s32[]{:T(128)}, f32[8,2048]{1,0:T(8,128)S(1)}, f32[8,2048]{1,0:T(8,128)S(1)}, f32[8,2048]{1,0:T(8,128)S(1)}, f32[8,2048]{1,0:T(8,128)S(1)}, /*index=5*/s32[]{:T(128)}) while((s32[]{:T(128)}, f32[8,2048]{1,0:T(8,128)S(1)}, f32[8,2048]{1,0:T(8,128)S(1)}, f32[8,2048]{1,0:T(8,128)S(1)}, f32[8,2048]{1,0:T(8,128)S(1)}, ...), condition=%wide.region_4.4_spmd, body=%wide.region_3.3_spmd.sunk | while | flops 573602 | bytes 934117 | solution.py:76
  836.8 15.0 %while.62 = (s32[]{:T(128)}, f32[8,2048]{1,0:T(8,128)S(1)}, f32[2,8,2048]{2,1,0:T(8,128)S(1)}, f32[8,2048]{1,0:T(8,128)S(1)}, f32[8,2048]{1,0:T(8,128)S(1)}, /*i...) while((s32[]{:T(128)}, f32[8,2048]{1,0:T(8,128)S(1)}, f32[2,8,2048]{2,1,0:T(8,128)S(1)}, ...), condition=%wide.region_7.8_spmd, body=%wide.region_6.7_spmd.sunk | while | flops 589986 | bytes 1065217 | solution.py:84
  (709 shorter events, 876.1 us)
Async XLA Ops:
  0.9 9.6 %collective-permute-start.7 = (f32[8,2048]{1,0:T(8,128)S(1)}, f32[8,2048]{1,0:T(8,128)S(1)}, u32[]{:S(2)}, u32[]{:S(2)}) collective-permute-start(f32[8,2048]{1,0:T(8,128)S(1)} %get-tuple-element.420), channel_id=1, source_target_pairs={{0,8},{8,16},{16,24},{24,32},{32,40},{40,48},{48,56},{56,64},{64,7... | collective-permute-start | bytes 196616 | tf_op jit(solution)/shard_map/ppermute | solution.py:25
  40.2 9.5 %collective-permute-start.16 = (f32[8,2048]{1,0:T(8,128)S(1)}, f32[8,2048]{1,0:T(8,128)S(1)}, u32[]{:S(2)}, u32[]{:S(2)}) collective-permute-start(f32[8,2048]{1,0:T(8,128)S(1)} %get-tuple-element.410), channel_id=1, source_target_pairs={{0,8},{8,16},{16,24},{24,32},{32,40},{40,48},{48,56},{56,64},{64,7... | collective-permute-start | bytes 196616 | tf_op jit(solution)/shard_map/ppermute | solution.py:25
  108.3 9.9 %collective-permute-start.6 = (f32[8,2048]{1,0:T(8,128)S(1)}, f32[8,2048]{1,0:T(8,128)S(1)}, u32[]{:S(2)}, u32[]{:S(2)}) collective-permute-start(f32[8,2048]{1,0:T(8,128)S(1)} %add.871), channel_id=1, source_target_pairs={{0,8},{8,16},{16,24},{24,32},{32,40},{40,48},{48,56},{56,64},{64,7... | collective-permute-start | bytes 196616 | tf_op jit(solution)/shard_map/while/body/eval_jaxpr/ppermute | solution.py:25
  132.6 10.2 %collective-permute-start.6 = (f32[8,2048]{1,0:T(8,128)S(1)}, f32[8,2048]{1,0:T(8,128)S(1)}, u32[]{:S(2)}, u32[]{:S(2)}) collective-permute-start(f32[8,2048]{1,0:T(8,128)S(1)} %add.871), channel_id=1, source_target_pairs={{0,8},{8,16},{16,24},{24,32},{32,40},{40,48},{48,56},{56,64},{64,7... | collective-permute-start | bytes 196616 | tf_op jit(solution)/shard_map/while/body/eval_jaxpr/ppermute | solution.py:25
  157.2 9.5 %collective-permute-start.6 = (f32[8,2048]{1,0:T(8,128)S(1)}, f32[8,2048]{1,0:T(8,128)S(1)}, u32[]{:S(2)}, u32[]{:S(2)}) collective-permute-start(f32[8,2048]{1,0:T(8,128)S(1)} %add.871), channel_id=1, source_target_pairs={{0,8},{8,16},{16,24},{24,32},{32,40},{40,48},{48,56},{56,64},{64,7... | collective-permute-start | bytes 196616 | tf_op jit(solution)/shard_map/while/body/eval_jaxpr/ppermute | solution.py:25
  181.2 9.5 %collective-permute-start.6 = (f32[8,2048]{1,0:T(8,128)S(1)}, f32[8,2048]{1,0:T(8,128)S(1)}, u32[]{:S(2)}, u32[]{:S(2)}) collective-permute-start(f32[8,2048]{1,0:T(8,128)S(1)} %add.871), channel_id=1, source_target_pairs={{0,8},{8,16},{16,24},{24,32},{32,40},{40,48},{48,56},{56,64},{64,7... | collective-permute-start | bytes 196616 | tf_op jit(solution)/shard_map/while/body/eval_jaxpr/ppermute | solution.py:25
  205.1 9.5 %collective-permute-start.6 = (f32[8,2048]{1,0:T(8,128)S(1)}, f32[8,2048]{1,0:T(8,128)S(1)}, u32[]{:S(2)}, u32[]{:S(2)}) collective-permute-start(f32[8,2048]{1,0:T(8,128)S(1)} %add.871), channel_id=1, source_target_pairs={{0,8},{8,16},{16,24},{24,32},{32,40},{40,48},{48,56},{56,64},{64,7... | collective-permute-start | bytes 196616 | tf_op jit(solution)/shard_map/while/body/eval_jaxpr/ppermute | solution.py:25
  229.0 9.5 %collective-permute-start.6 = (f32[8,2048]{1,0:T(8,128)S(1)}, f32[8,2048]{1,0:T(8,128)S(1)}, u32[]{:S(2)}, u32[]{:S(2)}) collective-permute-start(f32[8,2048]{1,0:T(8,128)S(1)} %add.871), channel_id=1, source_target_pairs={{0,8},{8,16},{16,24},{24,32},{32,40},{40,48},{48,56},{56,64},{64,7... | collective-permute-start | bytes 196616 | tf_op jit(solution)/shard_map/while/body/eval_jaxpr/ppermute | solution.py:25
  253.0 9.5 %collective-permute-start.6 = (f32[8,2048]{1,0:T(8,128)S(1)}, f32[8,2048]{1,0:T(8,128)S(1)}, u32[]{:S(2)}, u32[]{:S(2)}) collective-permute-start(f32[8,2048]{1,0:T(8,128)S(1)} %add.871), channel_id=1, source_target_pairs={{0,8},{8,16},{16,24},{24,32},{32,40},{40,48},{48,56},{56,64},{64,7... | collective-permute-start | bytes 196616 | tf_op jit(solution)/shard_map/while/body/eval_jaxpr/ppermute | solution.py:25
  276.9 9.5 %collective-permute-start.6 = (f32[8,2048]{1,0:T(8,128)S(1)}, f32[8,2048]{1,0:T(8,128)S(1)}, u32[]{:S(2)}, u32[]{:S(2)}) collective-permute-start(f32[8,2048]{1,0:T(8,128)S(1)} %add.871), channel_id=1, source_target_pairs={{0,8},{8,16},{16,24},{24,32},{32,40},{40,48},{48,56},{56,64},{64,7... | collective-permute-start | bytes 196616 | tf_op jit(solution)/shard_map/while/body/eval_jaxpr/ppermute | solution.py:25
  300.8 9.5 %collective-permute-start.6 = (f32[8,2048]{1,0:T(8,128)S(1)}, f32[8,2048]{1,0:T(8,128)S(1)}, u32[]{:S(2)}, u32[]{:S(2)}) collective-permute-start(f32[8,2048]{1,0:T(8,128)S(1)} %add.871), channel_id=1, source_target_pairs={{0,8},{8,16},{16,24},{24,32},{32,40},{40,48},{48,56},{56,64},{64,7... | collective-permute-start | bytes 196616 | tf_op jit(solution)/shard_map/while/body/eval_jaxpr/ppermute | solution.py:25
  324.8 9.5 %collective-permute-start.6 = (f32[8,2048]{1,0:T(8,128)S(1)}, f32[8,2048]{1,0:T(8,128)S(1)}, u32[]{:S(2)}, u32[]{:S(2)}) collective-permute-start(f32[8,2048]{1,0:T(8,128)S(1)} %add.871), channel_id=1, source_target_pairs={{0,8},{8,16},{16,24},{24,32},{32,40},{40,48},{48,56},{56,64},{64,7... | collective-permute-start | bytes 196616 | tf_op jit(solution)/shard_map/while/body/eval_jaxpr/ppermute | solution.py:25
  348.7 9.5 %collective-permute-start.6 = (f32[8,2048]{1,0:T(8,128)S(1)}, f32[8,2048]{1,0:T(8,128)S(1)}, u32[]{:S(2)}, u32[]{:S(2)}) collective-permute-start(f32[8,2048]{1,0:T(8,128)S(1)} %add.871), channel_id=1, source_target_pairs={{0,8},{8,16},{16,24},{24,32},{32,40},{40,48},{48,56},{56,64},{64,7... | collective-permute-start | bytes 196616 | tf_op jit(solution)/shard_map/while/body/eval_jaxpr/ppermute | solution.py:25
  372.6 9.5 %collective-permute-start.6 = (f32[8,2048]{1,0:T(8,128)S(1)}, f32[8,2048]{1,0:T(8,128)S(1)}, u32[]{:S(2)}, u32[]{:S(2)}) collective-permute-start(f32[8,2048]{1,0:T(8,128)S(1)} %add.871), channel_id=1, source_target_pairs={{0,8},{8,16},{16,24},{24,32},{32,40},{40,48},{48,56},{56,64},{64,7... | collective-permute-start | bytes 196616 | tf_op jit(solution)/shard_map/while/body/eval_jaxpr/ppermute | solution.py:25
  396.5 9.5 %collective-permute-start.6 = (f32[8,2048]{1,0:T(8,128)S(1)}, f32[8,2048]{1,0:T(8,128)S(1)}, u32[]{:S(2)}, u32[]{:S(2)}) collective-permute-start(f32[8,2048]{1,0:T(8,128)S(1)} %add.871), channel_id=1, source_target_pairs={{0,8},{8,16},{16,24},{24,32},{32,40},{40,48},{48,56},{56,64},{64,7... | collective-permute-start | bytes 196616 | tf_op jit(solution)/shard_map/while/body/eval_jaxpr/ppermute | solution.py:25
  420.5 9.5 %collective-permute-start.6 = (f32[8,2048]{1,0:T(8,128)S(1)}, f32[8,2048]{1,0:T(8,128)S(1)}, u32[]{:S(2)}, u32[]{:S(2)}) collective-permute-start(f32[8,2048]{1,0:T(8,128)S(1)} %add.871), channel_id=1, source_target_pairs={{0,8},{8,16},{16,24},{24,32},{32,40},{40,48},{48,56},{56,64},{64,7... | collective-permute-start | bytes 196616 | tf_op jit(solution)/shard_map/while/body/eval_jaxpr/ppermute | solution.py:25
  444.4 9.5 %collective-permute-start.6 = (f32[8,2048]{1,0:T(8,128)S(1)}, f32[8,2048]{1,0:T(8,128)S(1)}, u32[]{:S(2)}, u32[]{:S(2)}) collective-permute-start(f32[8,2048]{1,0:T(8,128)S(1)} %add.871), channel_id=1, source_target_pairs={{0,8},{8,16},{16,24},{24,32},{32,40},{40,48},{48,56},{56,64},{64,7... | collective-permute-start | bytes 196616 | tf_op jit(solution)/shard_map/while/body/eval_jaxpr/ppermute | solution.py:25
  468.3 9.5 %collective-permute-start.6 = (f32[8,2048]{1,0:T(8,128)S(1)}, f32[8,2048]{1,0:T(8,128)S(1)}, u32[]{:S(2)}, u32[]{:S(2)}) collective-permute-start(f32[8,2048]{1,0:T(8,128)S(1)} %add.871), channel_id=1, source_target_pairs={{0,8},{8,16},{16,24},{24,32},{32,40},{40,48},{48,56},{56,64},{64,7... | collective-permute-start | bytes 196616 | tf_op jit(solution)/shard_map/while/body/eval_jaxpr/ppermute | solution.py:25
  492.3 9.5 %collective-permute-start.6 = (f32[8,2048]{1,0:T(8,128)S(1)}, f32[8,2048]{1,0:T(8,128)S(1)}, u32[]{:S(2)}, u32[]{:S(2)}) collective-permute-start(f32[8,2048]{1,0:T(8,128)S(1)} %add.871), channel_id=1, source_target_pairs={{0,8},{8,16},{16,24},{24,32},{32,40},{40,48},{48,56},{56,64},{64,7... | collective-permute-start | bytes 196616 | tf_op jit(solution)/shard_map/while/body/eval_jaxpr/ppermute | solution.py:25
  516.2 9.5 %collective-permute-start.6 = (f32[8,2048]{1,0:T(8,128)S(1)}, f32[8,2048]{1,0:T(8,128)S(1)}, u32[]{:S(2)}, u32[]{:S(2)}) collective-permute-start(f32[8,2048]{1,0:T(8,128)S(1)} %add.871), channel_id=1, source_target_pairs={{0,8},{8,16},{16,24},{24,32},{32,40},{40,48},{48,56},{56,64},{64,7... | collective-permute-start | bytes 196616 | tf_op jit(solution)/shard_map/while/body/eval_jaxpr/ppermute | solution.py:25
  540.1 9.5 %collective-permute-start.6 = (f32[8,2048]{1,0:T(8,128)S(1)}, f32[8,2048]{1,0:T(8,128)S(1)}, u32[]{:S(2)}, u32[]{:S(2)}) collective-permute-start(f32[8,2048]{1,0:T(8,128)S(1)} %add.871), channel_id=1, source_target_pairs={{0,8},{8,16},{16,24},{24,32},{32,40},{40,48},{48,56},{56,64},{64,7... | collective-permute-start | bytes 196616 | tf_op jit(solution)/shard_map/while/body/eval_jaxpr/ppermute | solution.py:25
  564.1 9.5 %collective-permute-start.6 = (f32[8,2048]{1,0:T(8,128)S(1)}, f32[8,2048]{1,0:T(8,128)S(1)}, u32[]{:S(2)}, u32[]{:S(2)}) collective-permute-start(f32[8,2048]{1,0:T(8,128)S(1)} %add.871), channel_id=1, source_target_pairs={{0,8},{8,16},{16,24},{24,32},{32,40},{40,48},{48,56},{56,64},{64,7... | collective-permute-start | bytes 196616 | tf_op jit(solution)/shard_map/while/body/eval_jaxpr/ppermute | solution.py:25
  588.0 9.5 %collective-permute-start.6 = (f32[8,2048]{1,0:T(8,128)S(1)}, f32[8,2048]{1,0:T(8,128)S(1)}, u32[]{:S(2)}, u32[]{:S(2)}) collective-permute-start(f32[8,2048]{1,0:T(8,128)S(1)} %add.871), channel_id=1, source_target_pairs={{0,8},{8,16},{16,24},{24,32},{32,40},{40,48},{48,56},{56,64},{64,7... | collective-permute-start | bytes 196616 | tf_op jit(solution)/shard_map/while/body/eval_jaxpr/ppermute | solution.py:25
  611.9 9.5 %collective-permute-start.6 = (f32[8,2048]{1,0:T(8,128)S(1)}, f32[8,2048]{1,0:T(8,128)S(1)}, u32[]{:S(2)}, u32[]{:S(2)}) collective-permute-start(f32[8,2048]{1,0:T(8,128)S(1)} %add.871), channel_id=1, source_target_pairs={{0,8},{8,16},{16,24},{24,32},{32,40},{40,48},{48,56},{56,64},{64,7... | collective-permute-start | bytes 196616 | tf_op jit(solution)/shard_map/while/body/eval_jaxpr/ppermute | solution.py:25
  635.8 9.5 %collective-permute-start.6 = (f32[8,2048]{1,0:T(8,128)S(1)}, f32[8,2048]{1,0:T(8,128)S(1)}, u32[]{:S(2)}, u32[]{:S(2)}) collective-permute-start(f32[8,2048]{1,0:T(8,128)S(1)} %add.871), channel_id=1, source_target_pairs={{0,8},{8,16},{16,24},{24,32},{32,40},{40,48},{48,56},{56,64},{64,7... | collective-permute-start | bytes 196616 | tf_op jit(solution)/shard_map/while/body/eval_jaxpr/ppermute | solution.py:25
  659.8 9.5 %collective-permute-start.6 = (f32[8,2048]{1,0:T(8,128)S(1)}, f32[8,2048]{1,0:T(8,128)S(1)}, u32[]{:S(2)}, u32[]{:S(2)}) collective-permute-start(f32[8,2048]{1,0:T(8,128)S(1)} %add.871), channel_id=1, source_target_pairs={{0,8},{8,16},{16,24},{24,32},{32,40},{40,48},{48,56},{56,64},{64,7... | collective-permute-start | bytes 196616 | tf_op jit(solution)/shard_map/while/body/eval_jaxpr/ppermute | solution.py:25
  683.7 9.5 %collective-permute-start.6 = (f32[8,2048]{1,0:T(8,128)S(1)}, f32[8,2048]{1,0:T(8,128)S(1)}, u32[]{:S(2)}, u32[]{:S(2)}) collective-permute-start(f32[8,2048]{1,0:T(8,128)S(1)} %add.871), channel_id=1, source_target_pairs={{0,8},{8,16},{16,24},{24,32},{32,40},{40,48},{48,56},{56,64},{64,7... | collective-permute-start | bytes 196616 | tf_op jit(solution)/shard_map/while/body/eval_jaxpr/ppermute | solution.py:25
  707.6 9.5 %collective-permute-start.6 = (f32[8,2048]{1,0:T(8,128)S(1)}, f32[8,2048]{1,0:T(8,128)S(1)}, u32[]{:S(2)}, u32[]{:S(2)}) collective-permute-start(f32[8,2048]{1,0:T(8,128)S(1)} %add.871), channel_id=1, source_target_pairs={{0,8},{8,16},{16,24},{24,32},{32,40},{40,48},{48,56},{56,64},{64,7... | collective-permute-start | bytes 196616 | tf_op jit(solution)/shard_map/while/body/eval_jaxpr/ppermute | solution.py:25
  731.6 9.5 %collective-permute-start.6 = (f32[8,2048]{1,0:T(8,128)S(1)}, f32[8,2048]{1,0:T(8,128)S(1)}, u32[]{:S(2)}, u32[]{:S(2)}) collective-permute-start(f32[8,2048]{1,0:T(8,128)S(1)} %add.871), channel_id=1, source_target_pairs={{0,8},{8,16},{16,24},{24,32},{32,40},{40,48},{48,56},{56,64},{64,7... | collective-permute-start | bytes 196616 | tf_op jit(solution)/shard_map/while/body/eval_jaxpr/ppermute | solution.py:25
  755.5 9.5 %collective-permute-start.6 = (f32[8,2048]{1,0:T(8,128)S(1)}, f32[8,2048]{1,0:T(8,128)S(1)}, u32[]{:S(2)}, u32[]{:S(2)}) collective-permute-start(f32[8,2048]{1,0:T(8,128)S(1)} %add.871), channel_id=1, source_target_pairs={{0,8},{8,16},{16,24},{24,32},{32,40},{40,48},{48,56},{56,64},{64,7... | collective-permute-start | bytes 196616 | tf_op jit(solution)/shard_map/while/body/eval_jaxpr/ppermute | solution.py:25
  779.4 9.5 %collective-permute-start.6 = (f32[8,2048]{1,0:T(8,128)S(1)}, f32[8,2048]{1,0:T(8,128)S(1)}, u32[]{:S(2)}, u32[]{:S(2)}) collective-permute-start(f32[8,2048]{1,0:T(8,128)S(1)} %add.871), channel_id=1, source_target_pairs={{0,8},{8,16},{16,24},{24,32},{32,40},{40,48},{48,56},{56,64},{64,7... | collective-permute-start | bytes 196616 | tf_op jit(solution)/shard_map/while/body/eval_jaxpr/ppermute | solution.py:25
  803.4 9.5 %collective-permute-start.6 = (f32[8,2048]{1,0:T(8,128)S(1)}, f32[8,2048]{1,0:T(8,128)S(1)}, u32[]{:S(2)}, u32[]{:S(2)}) collective-permute-start(f32[8,2048]{1,0:T(8,128)S(1)} %add.871), channel_id=1, source_target_pairs={{0,8},{8,16},{16,24},{24,32},{32,40},{40,48},{48,56},{56,64},{64,7... | collective-permute-start | bytes 196616 | tf_op jit(solution)/shard_map/while/body/eval_jaxpr/ppermute | solution.py:25
  (155 other events, 792.6 us)
where the time goes:
time: 859 us; the launch traced here: 852 us
  starting transfers between devices  462 us (54%)
  waiting for transfers between devices  362 us (42%)
  other arithmetic  19.8 us (2%)
    ppermute x33, waiting for transfers between devices, shifted(): lax.ppermute(value, axis, [(source, source + steps) for source in range(i...  248 us
    ppermute x74, starting transfers between devices, padded_2(): lax.ppermute(lax.slice_in_dim(block, 0, width, axis=dim), axis, backward)  239 us
    ppermute x74, starting transfers between devices, padded_2(): lax.ppermute(lax.slice_in_dim(block, block.shape[dim] - width, None, axis...  157 us
    ppermute x74, waiting for transfers between devices, padded_2(): lax.ppermute(lax.slice_in_dim(block, 0, width, axis=dim), axis, backward)  82.8 us
    ppermute x33, starting transfers between devices, shifted(): lax.ppermute(value, axis, [(source, source + steps) for source in range(i...  65 us
    ppermute x74, waiting for transfers between devices, padded_2(): lax.ppermute(lax.slice_in_dim(block, block.shape[dim] - width, None, axis...  31.6 us
  transfers between devices with their start and end apart: 181, of which 107 were waited for; matrix products, arithmetic and copies ran while one was open for 0% of the time, Pallas kernels for 0%

commit v1 on v0

v1 whole, which is shorter than its diff:
```python
import functools

import jax
import jax.numpy as jnp
from jax import lax
from jax.experimental import pallas as pl
from jax.experimental.pallas import tpu as pltpu
from jax.sharding import PartitionSpec as P

M = 4
NZ = 8
NX_DEV = 4
NS = 8
STRIPS = 32
LANES = 128


def place_of(strip):
    chip, core = strip // 2, strip % 2
    y, q = chip // 4, chip % 4
    x = q + (y % 2) * (3 - 2 * q)
    return x, 2 * y + core


def strip_of(x, s):
    y, core = s // 2, s % 2
    q = x + (y % 2) * (3 - 2 * x)
    return 2 * (4 * y + q) + core


def lane_ids(rows):
    return lax.broadcasted_iota(jnp.int32, (rows, LANES), 1)


def pack_halves(value, out_ref):
    lane = lane_ids(16)
    for half in range(2):
        block = 1 + half
        packed = None
        for group in range(4):
            piece = value[16 * group : 16 * group + 16]
            shift = (32 * (group - block)) % LANES
            moved = piece if shift == 0 else pltpu.roll(piece, shift, 1)
            packed = moved if packed is None else jnp.where(lane < 32 * group, packed, moved)
        out_ref[half] = packed


def unpack_window(parts):
    lane = lane_ids(16)
    rows = []
    for group in range(4):
        row = None
        for block in range(4):
            shift = (32 * (block - group)) % LANES
            moved = parts[block] if shift == 0 else pltpu.roll(parts[block], shift, 1)
            row = moved if row is None else jnp.where(lane < 32 * block, row, moved)
        rows.append(row)
    return jnp.concatenate(rows, axis=0)


def stencil(cf, base, u):
    near = cf[base] * u + cf[base + 1] * pltpu.roll(u, 1, 0) + cf[base + 2] * pltpu.roll(u, 63, 0)
    return near + (cf[base + 3] * pltpu.roll(u, 1, 1) + cf[base + 4] * pltpu.roll(u, 127, 1))


def kernel(
    initial, source, rate, velx, vely, strengths, guess, out,
    amp, gb, fb, ib, sb, sp, rb, pb, cf, rx, rd, eb, pk, pe, lr, po, ob,
    ld, s1, r1, sq, rq, s2, r2, s3, r3,
):
    t, s = lax.axis_index("tm"), lax.axis_index("space")
    z, x = t // NX_DEV, t % NX_DEV
    c = strip_of(x, s)
    c_lo, c_hi = (c + STRIPS - 1) % STRIPS, (c + 1) % STRIPS
    zn = (z + 1) % NZ
    last_x = x == NX_DEV - 1

    def at(plane, strip):
        px, ps = place_of(strip)
        return (plane * NX_DEV + px, ps)

    barrier = pltpu.get_barrier_semaphore()

    def greet(device):
        pl.semaphore_signal(barrier, inc=1, device_id=device, device_id_type=pl.DeviceIdType.MESH)

    def greet_mate(i, _):
        greet(at(z, (c + i) % STRIPS))
        return 0

    lax.fori_loop(1, STRIPS, greet_mate, 0)

    def greet_before(i, _):
        greet((((z + NZ - 1) % NZ) * NX_DEV + NX_DEV - 1, i))
        return 0

    lax.fori_loop(0, NS, greet_before, 0)

    def greet_earlier(j, _):
        greet(at(z - j, c_lo))
        greet(at(z - j, c))
        greet(at(z - j, c_hi))
        return 0

    lax.fori_loop(1, 1 + jnp.minimum(z, 4), greet_earlier, 0)

    load_guess = pltpu.make_async_copy(guess, gb, ld.at[0])
    load_guess.start()
    load_amp = pltpu.make_async_copy(strengths, amp, ld.at[3])
    load_amp.start()
    for which, field in enumerate((rate, velx, vely, source)):

        @pl.when(x == which)
        def _(field=field):
            pltpu.make_async_copy(field, fb, ld.at[1]).start()

    @pl.when(jnp.logical_and(last_x, z == NZ - 1))
    def _():
        pltpu.make_async_copy(initial, ib, ld.at[2]).start()

    @pl.when(jnp.logical_and(last_x, z < NZ - 1))
    def _():
        pltpu.make_async_copy(guess.at[1], ib, ld.at[2]).start()

    load_guess.wait()
    load_amp.wait()
    pltpu.make_async_copy(rate, fb, ld.at[1]).wait()

    lane8 = lane_ids(8)

    def windows(tile_of, put):
        low = [pltpu.roll(tile_of(k), 32, 1) for k in range(16)]
        for k in range(16):
            put(2 * k, jnp.where(lane8 < 32, low[k - 1], low[k]))
        high = [pltpu.roll(tile_of(k), 96, 1) for k in range(16)]
        for k in range(16):
            put(2 * k + 1, jnp.where(lane8 < 96, high[k], high[(k + 1) % 16]))

    for i in range(2):

        def put_guess(strip, value, i=i):
            for m in range(M):
                value = jnp.where(lane8 == m, amp[M * i + m], value)
            sb[strip, i] = value

        windows(lambda k, i=i: gb[i, :, LANES * k : LANES * (k + 1)], put_guess)

    def put_field(strip, value):
        sb[strip, 2] = value

    windows(lambda k: fb[:, LANES * k : LANES * (k + 1)], put_field)

    @pl.when(last_x)
    def _():
        pltpu.make_async_copy(initial, ib, ld.at[2]).wait()

        def put_before(strip, value):
            sp[strip] = value

        windows(lambda k: ib[:, LANES * k : LANES * (k + 1)], put_before)

    pl.semaphore_wait(
        barrier, STRIPS - 1 + jnp.where(last_x, STRIPS, 0) + 3 * jnp.minimum(NZ - 1 - z, 4)
    )

    mine = rb.at[pl.ds(3 * x, 3), pl.ds(8 * s, 8)]

    @pl.when(last_x)
    def _():
        def send_before(i, _):
            strip = (c + i) % STRIPS
            pltpu.make_async_remote_copy(
                sp.at[strip], pb.at[pl.ds(8 * s, 8)], sq, rq, at(zn, strip), pl.DeviceIdType.MESH
            ).start()
            return 0

        lax.fori_loop(0, STRIPS, send_before, 0)

    def send_mate(i, _):
        strip = (c + i) % STRIPS
        pltpu.make_async_remote_copy(
            sb.at[strip], mine, s1, r1, at(z, strip), pl.DeviceIdType.MESH
        ).start()
        return 0

    lax.fori_loop(1, STRIPS, send_mate, 0)
    pltpu.make_async_copy(sb.at[c], mine, r1).start()
    pltpu.make_async_copy(rb, rb, r1).wait()

    d, a, b = rb[2], rb[5], rb[8]
    row = lax.broadcasted_iota(jnp.int32, (64, LANES), 0)
    col = lax.broadcasted_iota(jnp.int32, (64, LANES), 1) + (64 * c - 32)
    zero = jnp.zeros((64, LANES), jnp.float32)
    c_mid = 1.0 - (4.0 * d + (jnp.abs(a) + jnp.abs(b)))
    c_xm = jnp.where(row == 0, zero, d + jnp.maximum(a, 0.0))
    c_xp = jnp.where(row == 63, zero, d - jnp.minimum(a, 0.0))
    c_ym = jnp.where(col == 0, zero, d + jnp.maximum(b, 0.0))
    c_yp = jnp.where(col == 2047, zero, d - jnp.minimum(b, 0.0))
    cf[0], cf[1], cf[2], cf[3], cf[4] = c_mid, c_xm, c_xp, c_ym, c_yp
    cf[5] = 1.0 - float(M) * (4.0 * d + (jnp.abs(a) + jnp.abs(b)))
    cf[6], cf[7], cf[8], cf[9] = M * c_xm, M * c_xp, M * c_ym, M * c_yp

    pltpu.make_async_copy(pb, pb, rq).wait()

    def forced(u, tile, m):
        strength = jnp.broadcast_to(rb[tile, 0:8, m : m + 1], (8, LANES))
        push = rb[11].reshape(8, 8, LANES) * strength[None]
        return stencil(cf, 0, u) + push.reshape(64, LANES)

    def fine_pair(xx, first):
        tile = 3 * xx
        u, v = first, rb[tile]
        for m in range(M):
            u = forced(u, tile, m)
            v = forced(v, tile + 1, m)
        rx[2 * xx], rx[2 * xx + 1] = u, v
        u, v = u - rb[tile], v - rb[tile + 1]
        for m in range(M):
            u = stencil(cf, 0, u)
            v = stencil(cf, 0, v)
        rd[2 * xx], rd[2 * xx + 1] = u, v
        return rb[tile + 1]

    lax.fori_loop(0, NX_DEV, fine_pair, pb[...])

    def coarse_local(k, err):
        return stencil(cf, 5, err) + rd[k]

    def coarse_power(err):
        return lax.fori_loop(0, 8, lambda k, v: stencil(cf, 5, v), err)

    entry = jnp.where(z == 0, rx[0] - rx[0], zero)
    eb[...] = entry
    local_last = lax.fori_loop(0, 8, coarse_local, entry)
    pack_halves(local_last, pk)

    def send_three(packed, plane, slot):
        for src, dst, strip in ((packed, lr.at[slot, pl.ds(1, 2)], c), (packed.at[0], lr.at[slot, 3], c_lo), (packed.at[1], lr.at[slot, 0], c_hi)):
            pltpu.make_async_remote_copy(
                src, dst, s2.at[slot], r2.at[slot], at(plane, strip), pl.DeviceIdType.MESH
            ).start()

    @pl.when(z == 0)
    def _():
        send_three(pk, z + 4, 0)

    for j in range(3, 0, -1):

        @pl.when(z + j < NZ)
        def _(j=j):
            send_three(pk, z + j, j)

    @pl.when(z >= 4)
    def _():
        pltpu.make_async_copy(lr.at[0], lr.at[0], r2.at[0]).wait()
        eb[...] = unpack_window([lr[0, h] for h in range(4)])

    for j in range(3, 0, -1):

        @pl.when(z - j >= 0)
        def _(j=j):
            pltpu.make_async_copy(lr.at[j], lr.at[j], r2.at[j]).wait()
            part = unpack_window([lr[j, h] for h in range(4)])
            steps = jnp.where(z - j > 0, 8, 0)
            eb[...] = part + lax.fori_loop(0, steps, lambda k, v: stencil(cf, 5, v), eb[...])

    lane64 = lane_ids(64)
    err = eb[...]
    for xx in range(NX_DEV):
        first = rx[2 * xx] + err
        err = coarse_local(2 * xx, err)
        second = rx[2 * xx + 1] + err
        err = coarse_local(2 * xx + 1, err)
        po[xx] = jnp.where(lane64 < 64, pltpu.roll(first, 96, 1), pltpu.roll(second, 32, 1))

    @pl.when(jnp.logical_and(z >= 1, z <= 3))
    def _():
        pack_halves(err, pe)
        send_three(pe, z + 4, 0)

    def send_out(i, _):
        xx, ss = place_of((c + i) % STRIPS)
        pltpu.make_async_remote_copy(
            po.at[xx, pl.ds(8 * ss, 8)], ob.at[c], s3, r3, (z * NX_DEV + xx, ss), pl.DeviceIdType.MESH
        ).start()
        return 0

    lax.fori_loop(1, STRIPS, send_out, 0)
    pltpu.make_async_copy(po.at[x, pl.ds(8 * s, 8)], ob.at[c], r3).start()
    pltpu.make_async_copy(ob, ob, r3).wait()

    for p in range(16):
        left, right = ob[2 * p], ob[2 * p + 1]
        here = slice(LANES * p, LANES * (p + 1))
        out[0, :, here] = jnp.where(lane8 < 64, left, pltpu.roll(right, 64, 1))
        out[1, :, here] = jnp.where(lane8 < 64, pltpu.roll(left, 64, 1), right)

    sent = sb.at[pl.ds(0, STRIPS - 1)]
    pltpu.make_async_copy(sent, sent, s1).wait()

    @pl.when(last_x)
    def _():
        pltpu.make_async_copy(sp, sp, sq).wait()

    @pl.when(z <= 3)
    def _():
        pltpu.make_async_copy(lr.at[0], lr.at[0], s2.at[0]).wait()

    for j in range(1, 4):

        @pl.when(z + j < NZ)
        def _(j=j):
            pltpu.make_async_copy(lr.at[j], lr.at[j], s2.at[j]).wait()

    gone = ob.at[pl.ds(0, STRIPS - 1)]
    pltpu.make_async_copy(gone, gone, s3).wait()


def per_device(*blocks):
    any_space = pl.BlockSpec(memory_space=pl.ANY)
    f32 = functools.partial(pltpu.VMEM, dtype=jnp.float32)
    sem = pltpu.SemaphoreType.DMA
    return pl.pallas_call(
        kernel,
        out_shape=jax.ShapeDtypeStruct((2, 8, 2048), jnp.float32),
        in_specs=[any_space] * 7,
        out_specs=pl.BlockSpec(memory_space=pltpu.VMEM),
        scratch_shapes=[
            pltpu.SMEM((8,), jnp.float32),
            f32((2, 8, 2048)),
            f32((8, 2048)),
            f32((8, 2048)),
            f32((STRIPS, 3, 8, LANES)),
            f32((STRIPS, 8, LANES)),
            f32((12, 64, LANES)),
            f32((64, LANES)),
            f32((10, 64, LANES)),
            f32((8, 64, LANES)),
            f32((8, 64, LANES)),
            f32((64, LANES)),
            f32((2, 16, LANES)),
            f32((2, 16, LANES)),
            f32((4, 4, 16, LANES)),
            f32((NX_DEV, 64, LANES)),
            f32((STRIPS, 8, LANES)),
            sem((4,)),
            sem,
            sem,
            sem,
            sem,
            sem((4,)),
            sem((4,)),
            sem,
            sem,
        ],
        compiler_params=pltpu.CompilerParams(
            collective_id=0, has_side_effects=True, vmem_limit_bytes=56 * 1024 * 1024
        ),
        cost_estimate=pl.CostEstimate(flops=20_000_000, bytes_accessed=700_000, transcendentals=0),
        name="cycle",
    )(*blocks)


def solution(mesh):
    in_specs = (
        P("space", None),
        P("space", None),
        P("space", None),
        P("space", None),
        P("space", None),
        P("tm"),
        P("tm", "space", None),
    )
    out_specs = P("tm", "space", None)
    return jax.shard_map(
        per_device, mesh=mesh, in_specs=in_specs, out_specs=out_specs, check_vma=False
    )
```

time: 859 us -> 44.5 us (0.05)
  the two profiles are of different devices: /device:TPU:144 before, /device:TPU:225 now
where the time goes in v1:
time: 44.5 us; the launch traced here: 44.4 us
  Pallas kernels  42.8 us (96%)
  local copies, waits for them, and re-layouts  1.57 us (4%)
    pallas_call x1, Pallas kernels, per_device(): pl.pallas_call(kernel, out_shape=jax.ShapeDtypeStruct((2, 8, 2048), jnp.f...  42.8 us
    unnamed x1, local copies, waits for them, and re-layouts  1.57 us

profile of v1, /device:TPU:225, one launch (start us, length us, event | category | flops | bytes accessed | tf_op | source)
XLA Modules:
  0.0 44.4 jit_solution(10335242418007533277)
XLA Ops:
  0.0 42.8 %cycle.1 = f32[2,8,2048]{2,1,0:T(8,128)} custom-call(f32[8,2048]{1,0:T(8,128)} %initial.1, f32[8,2048]{1,0:T(8,128)} %source.1, f32[8,2048]{1,0:T(8,128)} %rate.1, f32[8,2048]{1,0:T(8,128)} %velx.1, f32[8,2048]{1,0:T(8,128)} %vely.1, f32[8]{0:T(128)} %strengths.1, f32[2,8,2048]{2,1,0:T(8,128)} %guess.1), custom_call_target="tpu_custom_call" | custom-call | flops 20000000 | bytes 700000 | tf_op jit(solution)/shard_map/cycle/pallas_call | solution.py:323
  42.8 1.6 %copy.9 = f32[2,8,2048]{2,1,0:T(8,128)} copy(f32[2,8,2048]{2,1,0:T(8,128)} %cycle.1) | data formatting | bytes 262144

commit v2 on v1

--- a/solution.py
+++ b/solution.py
@@ -58,14 +58,44 @@
     return jnp.concatenate(rows, axis=0)
 
 
+def point(cf, base, mid, left, right):
+    near = cf[base] * mid + cf[base + 1] * pltpu.roll(mid, 1, 0) + cf[base + 2] * pltpu.roll(mid, 63, 0)
+    return near + (cf[base + 3] * left + cf[base + 4] * right)
+
+
+def lanes(u, steps):
+    return pltpu.roll(u, steps % LANES, 1)
+
+
 def stencil(cf, base, u):
-    near = cf[base] * u + cf[base + 1] * pltpu.roll(u, 1, 0) + cf[base + 2] * pltpu.roll(u, 63, 0)
-    return near + (cf[base + 3] * pltpu.roll(u, 1, 1) + cf[base + 4] * pltpu.roll(u, 127, 1))
+    return point(cf, base, u, lanes(u, 1), lanes(u, -1))
+
+
+def coarse_two(cf, u, r1=None, r2=None):
+    left, left2, right, right2 = lanes(u, 1), lanes(u, 2), lanes(u, -1), lanes(u, -2)
+    v = point(cf, 5, u, left, right)
+    v_left = point(cf, 10, left, left2, u)
+    v_right = point(cf, 15, right, u, right2)
+    if r1 is not None:
+        v, v_left, v_right = v + r1, v_left + lanes(r1, 1), v_right + lanes(r1, -1)
+    w = point(cf, 5, v, v_left, v_right)
+    if r2 is not None:
+        w = w + r2
+    return v, w
+
+
+def coarse_eight(cf, u):
+    def body(i, u):
+        for _ in range(2):
+            u = coarse_two(cf, u)[1]
+        return u
+
+    return lax.fori_loop(0, 2, body, u)
 
 
 def kernel(
-    initial, source, rate, velx, vely, strengths, guess, out,
-    amp, gb, fb, ib, sb, sp, rb, pb, cf, rx, rd, eb, pk, pe, lr, po, ob,
+    initial, source, rate, velx, vely, strengths, guess, ob,
+    amp, gb, fb, ib, sb, sp, rb, pb, cf, rx, rd, eb, pk, pe, lr, ul, po,
     ld, s1, r1, sq, rq, s2, r2, s3, r3,
 ):
     t, s = lax.axis_index("tm"), lax.axis_index("space")
@@ -96,13 +126,25 @@
 
     lax.fori_loop(0, NS, greet_before, 0)
 
-    def greet_earlier(j, _):
-        greet(at(z - j, c_lo))
-        greet(at(z - j, c))
-        greet(at(z - j, c_hi))
+    def greet_three(plane):
+        greet(at(plane, c_lo))
+        greet(at(plane, c))
+        greet(at(plane, c_hi))
+
+    @pl.when(z == 0)
+    def _():
+        for j in range(1, 4):
+            greet_three(j)
+
+    @pl.when(z > 0)
+    def _():
+        greet_three(0)
+
+    def greet_upper(j, _):
+        greet_three(j)
         return 0
 
-    lax.fori_loop(1, 1 + jnp.minimum(z, 4), greet_earlier, 0)
+    lax.fori_loop(4, jnp.maximum(z, 4), greet_upper, 0)
 
     load_guess = pltpu.make_async_copy(guess, gb, ld.at[0])
     load_guess.start()
@@ -159,8 +201,9 @@
 
         windows(lambda k: ib[:, LANES * k : LANES * (k + 1)], put_before)
 
+    fan = jnp.where(z == 0, NZ - 1, jnp.where(z < 4, 1, NZ - 1 - z))
     pl.semaphore_wait(
-        barrier, STRIPS - 1 + jnp.where(last_x, STRIPS, 0) + 3 * jnp.minimum(NZ - 1 - z, 4)
+        barrier, STRIPS - 1 + jnp.where(last_x, STRIPS, 0) + 3 * fan
     )
 
     mine = rb.at[pl.ds(3 * x, 3), pl.ds(8 * s, 8)]
@@ -199,6 +242,9 @@
     cf[0], cf[1], cf[2], cf[3], cf[4] = c_mid, c_xm, c_xp, c_ym, c_yp
     cf[5] = 1.0 - float(M) * (4.0 * d + (jnp.abs(a) + jnp.abs(b)))
     cf[6], cf[7], cf[8], cf[9] = M * c_xm, M * c_xp, M * c_ym, M * c_yp
+    for k in range(5):
+        cf[10 + k] = lanes(cf[5 + k], 1)
+        cf[15 + k] = lanes(cf[5 + k], -1)
 
     pltpu.make_async_copy(pb, pb, rq).wait()
 
@@ -207,124 +253,155 @@
         push = rb[11].reshape(8, 8, LANES) * strength[None]
         return stencil(cf, 0, u) + push.reshape(64, LANES)
 
-    def fine_pair(xx, first):
-        tile = 3 * xx
-        u, v = first, rb[tile]
-        for m in range(M):
-            u = forced(u, tile, m)
-            v = forced(v, tile + 1, m)
-        rx[2 * xx], rx[2 * xx + 1] = u, v
-        u, v = u - rb[tile], v - rb[tile + 1]
-        for m in range(M):
-            u = stencil(cf, 0, u)
-            v = stencil(cf, 0, v)
-        rd[2 * xx], rd[2 * xx + 1] = u, v
-        return rb[tile + 1]
-
-    lax.fori_loop(0, NX_DEV, fine_pair, pb[...])
-
-    def coarse_local(k, err):
-        return stencil(cf, 5, err) + rd[k]
-
-    def coarse_power(err):
-        return lax.fori_loop(0, 8, lambda k, v: stencil(cf, 5, v), err)
+    tiles = [3 * (k // 2) + k % 2 for k in range(8)]
+    state = [pb[...]] + [rb[tile] for tile in tiles[:-1]]
+    for m in range(M):
+        state = [forced(u, tile, m) for u, tile in zip(state, tiles)]
+    for k in range(8):
+        rx[k] = state[k]
+    state = [u - rb[tile] for u, tile in zip(state, tiles)]
+    for m in range(M):
+        state = [stencil(cf, 0, u) for u in state]
+    for k in range(8):
+        rd[k] = state[k]
 
     entry = jnp.where(z == 0, rx[0] - rx[0], zero)
-    eb[...] = entry
-    local_last = lax.fori_loop(0, 8, coarse_local, entry)
+    local_last = entry
+    for k in range(0, 8, 2):
+        local_last = coarse_two(cf, local_last, rd[k], rd[k + 1])[1]
     pack_halves(local_last, pk)
 
-    def send_three(packed, plane, slot):
-        for src, dst, strip in ((packed, lr.at[slot, pl.ds(1, 2)], c), (packed.at[0], lr.at[slot, 3], c_lo), (packed.at[1], lr.at[slot, 0], c_hi)):
+    def send_main(packed, plane, slot, sem):
+        pltpu.make_async_remote_copy(
+            packed, lr.at[slot, pl.ds(1, 2)], s2.at[sem], r2.at[slot], at(plane, c), pl.DeviceIdType.MESH
+        ).start()
+
+    def send_sides(packed, plane, slot, sem):
+        for src, part, strip in ((packed.at[0], 3, c_lo), (packed.at[1], 0, c_hi)):
             pltpu.make_async_remote_copy(
-                src, dst, s2.at[slot], r2.at[slot], at(plane, strip), pl.DeviceIdType.MESH
+                src, lr.at[slot, part], s2.at[sem], r2.at[slot], at(plane, strip), pl.DeviceIdType.MESH
             ).start()
 
+    def send_three(packed, plane, slot, sem):
+        send_main(packed, plane, slot, sem)
+        send_sides(packed, plane, slot, sem)
+
+    def arrived(slot):
+        pltpu.make_async_copy(lr.at[slot], lr.at[slot], r2.at[slot]).wait()
+        return unpack_window([lr[slot, h] for h in range(4)])
+
     @pl.when(z == 0)
     def _():
-        send_three(pk, z + 4, 0)
-
-    for j in range(3, 0, -1):
-
-        @pl.when(z + j < NZ)
+        send_sides(pk, 0, 0, 0)
+        pltpu.make_async_copy(pk, lr.at[0, pl.ds(1, 2)], r2.at[0]).start()
+        send_three(pk, 1, 0, 1)
+        e = arrived(0)
+        for j in range(1, 4):
+            e = coarse_eight(cf, e) + arrived(j)
+            if j == 3:
+                pack_halves(e, pe.at[3])
+                for plane in (7, 6, 5, 4):
+                    send_three(pe.at[3], plane, 0, plane)
+            else:
+                pack_halves(e, pe.at[j])
+        for plane in (3, 2):
+            send_three(pe.at[plane - 1], plane, 0, plane)
+        eb[...] = entry
+
+    @pl.when(jnp.logical_and(z >= 1, z <= 3))
+    def _():
+        send_three(pk, 0, z, 1)
+
+    for plane in (7, 6, 5):
+
+        @pl.when(jnp.logical_and(z >= 4, z < plane))
+        def _(plane=plane):
+            send_three(pk, plane, z - 3, plane)
+
+    for j in range(4, 7):
+
+        @pl.when(z > j)
         def _(j=j):
-            send_three(pk, z + j, j)
-
-    @pl.when(z >= 4)
-    def _():
-        pltpu.make_async_copy(lr.at[0], lr.at[0], r2.at[0]).wait()
-        eb[...] = unpack_window([lr[0, h] for h in range(4)])
-
-    for j in range(3, 0, -1):
-
-        @pl.when(z - j >= 0)
-        def _(j=j):
-            pltpu.make_async_copy(lr.at[j], lr.at[j], r2.at[j]).wait()
-            part = unpack_window([lr[j, h] for h in range(4)])
-            steps = jnp.where(z - j > 0, 8, 0)
-            eb[...] = part + lax.fori_loop(0, steps, lambda k, v: stencil(cf, 5, v), eb[...])
+            ul[j - 4] = arrived(j - 3)
+
+    @pl.when(z >= 1)
+    def _():
+        eb[...] = lax.fori_loop(0, jnp.maximum(z - 4, 0), lambda j, e: coarse_eight(cf, e) + ul[j], arrived(0))
 
     lane64 = lane_ids(64)
     err = eb[...]
     for xx in range(NX_DEV):
         first = rx[2 * xx] + err
-        err = coarse_local(2 * xx, err)
-        second = rx[2 * xx + 1] + err
-        err = coarse_local(2 * xx + 1, err)
+        mid, err = coarse_two(cf, err, rd[2 * xx], rd[2 * xx + 1])
+        second = rx[2 * xx + 1] + mid
         po[xx] = jnp.where(lane64 < 64, pltpu.roll(first, 96, 1), pltpu.roll(second, 32, 1))
 
+        def send_out(i, _, xx=xx):
+            ss = (s + i) % NS
+            rows = po.at[xx, pl.ds(8 * ss, 8)]
+            own = jnp.logical_and(xx == x, i == 0)
+
+            @pl.when(own)
+            def _():
+                pltpu.make_async_copy(rows, ob.at[c], r3).start()
+
+            @pl.when(jnp.logical_not(own))
+            def _():
+                pltpu.make_async_remote_copy(
+                    rows, ob.at[c], s3, r3, (z * NX_DEV + xx, ss), pl.DeviceIdType.MESH
+                ).start()
+
+            return 0
+
+        lax.fori_loop(0, NS, send_out, 0)
+
+    pltpu.make_async_copy(ob, ob, r3).wait()
+
+    sent = sb.at[pl.ds(0, STRIPS - 1)]
+    pltpu.make_async_copy(sent, sent, s1).wait()
+
+    @pl.when(last_x)
+    def _():
+        pltpu.make_async_copy(sp, sp, sq).wait()
+
+    @pl.when(z == 0)
+    def _():
+        pltpu.make_async_copy(pk, pk, s2.at[0]).wait()
+        for plane in range(1, NZ):
+            pltpu.make_async_copy(lr.at[0], lr.at[0], s2.at[plane]).wait()
+
     @pl.when(jnp.logical_and(z >= 1, z <= 3))
     def _():
-        pack_halves(err, pe)
-        send_three(pe, z + 4, 0)
-
-    def send_out(i, _):
-        xx, ss = place_of((c + i) % STRIPS)
-        pltpu.make_async_remote_copy(
-            po.at[xx, pl.ds(8 * ss, 8)], ob.at[c], s3, r3, (z * NX_DEV + xx, ss), pl.DeviceIdType.MESH
-        ).start()
-        return 0
-
-    lax.fori_loop(1, STRIPS, send_out, 0)
-    pltpu.make_async_copy(po.at[x, pl.ds(8 * s, 8)], ob.at[c], r3).start()
-    pltpu.make_async_copy(ob, ob, r3).wait()
-
+        pltpu.make_async_copy(lr.at[0], lr.at[0], s2.at[1]).wait()
+
+    for plane in (7, 6, 5):
+
+        @pl.when(jnp.logical_and(z >= 4, z < plane))
+        def _(plane=plane):
+            pltpu.make_async_copy(lr.at[0], lr.at[0], s2.at[plane]).wait()
+
+    gone = ob.at[pl.ds(0, STRIPS - 1)]
+    pltpu.make_async_copy(gone, gone, s3).wait()
+
+
+def place_rows(ob, out):
+    lane8 = lane_ids(8)
     for p in range(16):
         left, right = ob[2 * p], ob[2 * p + 1]
         here = slice(LANES * p, LANES * (p + 1))
         out[0, :, here] = jnp.where(lane8 < 64, left, pltpu.roll(right, 64, 1))
         out[1, :, here] = jnp.where(lane8 < 64, pltpu.roll(left, 64, 1), right)
 
-    sent = sb.at[pl.ds(0, STRIPS - 1)]
-    pltpu.make_async_copy(sent, sent, s1).wait()
-
-    @pl.when(last_x)
-    def _():
-        pltpu.make_async_copy(sp, sp, sq).wait()
-
-    @pl.when(z <= 3)
-    def _():
-        pltpu.make_async_copy(lr.at[0], lr.at[0], s2.at[0]).wait()
-
-    for j in range(1, 4):
-
-        @pl.when(z + j < NZ)
-        def _(j=j):
-            pltpu.make_async_copy(lr.at[j], lr.at[j], s2.at[j]).wait()
-
-    gone = ob.at[pl.ds(0, STRIPS - 1)]
-    pltpu.make_async_copy(gone, gone, s3).wait()
-
 
 def per_device(*blocks):
     any_space = pl.BlockSpec(memory_space=pl.ANY)
     f32 = functools.partial(pltpu.VMEM, dtype=jnp.float32)
     sem = pltpu.SemaphoreType.DMA
-    return pl.pallas_call(
+    strips = pl.pallas_call(
         kernel,
-        out_shape=jax.ShapeDtypeStruct((2, 8, 2048), jnp.float32),
+        out_shape=jax.ShapeDtypeStruct((STRIPS, 8, LANES), jnp.float32),
         in_specs=[any_space] * 7,
-        out_specs=pl.BlockSpec(memory_space=pltpu.VMEM),
+        out_specs=any_space,
         scratch_shapes=[
             pltpu.SMEM((8,), jnp.float32),
             f32((2, 8, 2048)),
@@ -334,21 +411,21 @@
             f32((STRIPS, 8, LANES)),
             f32((12, 64, LANES)),
             f32((64, LANES)),
-            f32((10, 64, LANES)),
+            f32((20, 64, LANES)),
             f32((8, 64, LANES)),
             f32((8, 64, LANES)),
             f32((64, LANES)),
             f32((2, 16, LANES)),
-            f32((2, 16, LANES)),
+            f32((4, 2, 16, LANES)),
             f32((4, 4, 16, LANES)),
+            f32((3, 64, LANES)),
             f32((NX_DEV, 64, LANES)),
-            f32((STRIPS, 8, LANES)),
             sem((4,)),
             sem,
             sem,
             sem,
             sem,
-            sem((4,)),
+            sem((8,)),
             sem((4,)),
             sem,
             sem,
@@ -359,6 +436,14 @@
         cost_estimate=pl.CostEstimate(flops=20_000_000, bytes_accessed=700_000, transcendentals=0),
         name="cycle",
     )(*blocks)
+    in_vmem = pl.BlockSpec(memory_space=pltpu.VMEM)
+    return pl.pallas_call(
+        place_rows,
+        out_shape=jax.ShapeDtypeStruct((2, 8, 2048), jnp.float32),
+        in_specs=[in_vmem],
+        out_specs=in_vmem,
+        name="place",
+    )(strips)
 
 
 def solution(mesh):

time: 44.5 us -> 36.2 us (0.81)
  the two profiles are of different devices: /device:TPU:225 before, /device:TPU:65 now
where the time goes in v2:
time: 36.2 us; the launch traced here: 36.1 us
  Pallas kernels  36.1 us (100%)
    pallas_call x1, Pallas kernels, per_device(): pl.pallas_call(kernel, out_shape=jax.ShapeDtypeStruct((STRIPS, 8, LANES),...  34.4 us
    pallas_call x1, Pallas kernels, per_device(): pl.pallas_call(place_rows, out_shape=jax.ShapeDtypeStruct((2, 8, 2048), j...  1.66 us

profile of v2, /device:TPU:65, one launch (start us, length us, event | category | flops | bytes accessed | tf_op | source)
XLA Modules:
  0.0 36.1 jit_solution(15620613621448874886)
XLA Ops:
  0.0 34.4 %cycle.1.ob = f32[32,8,128]{2,1,0:T(8,128)} custom-call(f32[8,2048]{1,0:T(8,128)} %initial.1, f32[8,2048]{1,0:T(8,128)} %source.1, f32[8,2048]{1,0:T(8,128)} %rate.1, f32[8,2048]{1,0:T(8,128)} %velx.1, f32[8,2048]{1,0:T(8,128)} %vely.1, f32[8]{0:T(128)} %strengths.1, f32[2,8,2048]{2,1,0:T(8,128)} %guess.1), custom_call_target="tpu_custom_call" | custom-call | flops 20000000 | bytes 700000 | tf_op jit(solution)/shard_map/cycle/pallas_call | solution.py:400
  34.4 1.7 %place.1 = f32[2,8,2048]{2,1,0:T(8,128)} custom-call(f32[32,8,128]{2,1,0:T(8,128)} %cycle.1.ob), custom_call_target="tpu_custom_call" | custom-call | tf_op jit(solution)/shard_map/place/pallas_call | solution.py:440

commit v3 on v2

--- a/solution.py
+++ b/solution.py
@@ -95,15 +95,16 @@
 
 def kernel(
     initial, source, rate, velx, vely, strengths, guess, ob,
-    amp, gb, fb, ib, sb, sp, rb, pb, cf, rx, rd, eb, pk, pe, lr, ul, po,
-    ld, s1, r1, sq, rq, s2, r2, s3, r3,
+    amp, gb, fb, ib, sb, sp, rb, pb, cf, rx, rd, pk, pe, lr, ul, lw, e_in, po,
+    ld, s1, r1, sq, rq, s2, r2, r4, s3, r3, ready,
 ):
     t, s = lax.axis_index("tm"), lax.axis_index("space")
     z, x = t // NX_DEV, t % NX_DEV
     c = strip_of(x, s)
     c_lo, c_hi = (c + STRIPS - 1) % STRIPS, (c + 1) % STRIPS
-    zn = (z + 1) % NZ
-    last_x = x == NX_DEV - 1
+    gives_next = jnp.logical_and(x == NX_DEV - 1, z < NZ - 1)
+    gives_first = jnp.logical_and(x == 0, z == 0)
+    gives = jnp.logical_or(gives_next, gives_first)
 
     def at(plane, strip):
         px, ps = place_of(strip)
@@ -121,10 +122,10 @@
     lax.fori_loop(1, STRIPS, greet_mate, 0)
 
     def greet_before(i, _):
-        greet((((z + NZ - 1) % NZ) * NX_DEV + NX_DEV - 1, i))
+        greet(((z - 1) * NX_DEV + NX_DEV - 1, i))
         return 0
 
-    lax.fori_loop(0, NS, greet_before, 0)
+    lax.fori_loop(0, jnp.where(z > 0, NS, 0), greet_before, 0)
 
     def greet_three(plane):
         greet(at(plane, c_lo))
@@ -133,18 +134,21 @@
 
     @pl.when(z == 0)
     def _():
-        for j in range(1, 4):
-            greet_three(j)
-
-    @pl.when(z > 0)
-    def _():
-        greet_three(0)
-
-    def greet_upper(j, _):
-        greet_three(j)
+        for plane in range(1, 4):
+            greet(at(plane, c))
+        for plane in range(4, NZ):
+            greet_three(plane)
+
+    def greet_upper(plane, _):
+        greet(at(plane, c))
         return 0
 
     lax.fori_loop(4, jnp.maximum(z, 4), greet_upper, 0)
+
+    @pl.when(z == 7)
+    def _():
+        greet(at(4, c_lo))
+        greet(at(4, c_hi))
 
     load_guess = pltpu.make_async_copy(guess, gb, ld.at[0])
     load_guess.start()
@@ -156,11 +160,11 @@
         def _(field=field):
             pltpu.make_async_copy(field, fb, ld.at[1]).start()
 
-    @pl.when(jnp.logical_and(last_x, z == NZ - 1))
+    @pl.when(gives_first)
     def _():
         pltpu.make_async_copy(initial, ib, ld.at[2]).start()
 
-    @pl.when(jnp.logical_and(last_x, z < NZ - 1))
+    @pl.when(gives_next)
     def _():
         pltpu.make_async_copy(guess.at[1], ib, ld.at[2]).start()
 
@@ -192,7 +196,7 @@
 
     windows(lambda k: fb[:, LANES * k : LANES * (k + 1)], put_field)
 
-    @pl.when(last_x)
+    @pl.when(gives)
     def _():
         pltpu.make_async_copy(initial, ib, ld.at[2]).wait()
 
@@ -201,23 +205,44 @@
 
         windows(lambda k: ib[:, LANES * k : LANES * (k + 1)], put_before)
 
-    fan = jnp.where(z == 0, NZ - 1, jnp.where(z < 4, 1, NZ - 1 - z))
-    pl.semaphore_wait(
-        barrier, STRIPS - 1 + jnp.where(last_x, STRIPS, 0) + 3 * fan
-    )
+    hubs = jnp.where(z == 0, 0, jnp.where(z < 4, 1, 3))
+    uppers = jnp.where(z == 4, 5, jnp.where(z == 5, 2, jnp.where(z == 6, 1, 0)))
+    pl.semaphore_wait(barrier, STRIPS - 1 + jnp.where(gives_next, STRIPS, 0) + hubs + uppers)
+
+    def signal_ready(strip):
+        pl.semaphore_signal(
+            ready.at[z], inc=1, device_id=at(0, strip), device_id_type=pl.DeviceIdType.MESH
+        )
+
+    @pl.when(z > 0)
+    def _():
+        signal_ready(c)
+
+    @pl.when(z >= 4)
+    def _():
+        signal_ready(c_lo)
+        signal_ready(c_hi)
 
     mine = rb.at[pl.ds(3 * x, 3), pl.ds(8 * s, 8)]
 
-    @pl.when(last_x)
-    def _():
+    ahead = pb.at[pl.ds(8 * s, 8)]
+
+    @pl.when(gives)
+    def _():
+        to = jnp.where(gives_next, z + 1, 0)
+
         def send_before(i, _):
             strip = (c + i) % STRIPS
             pltpu.make_async_remote_copy(
-                sp.at[strip], pb.at[pl.ds(8 * s, 8)], sq, rq, at(zn, strip), pl.DeviceIdType.MESH
+                sp.at[strip], ahead, sq, rq, at(to, strip), pl.DeviceIdType.MESH
             ).start()
             return 0
 
-        lax.fori_loop(0, STRIPS, send_before, 0)
+        lax.fori_loop(jnp.where(gives_next, 0, 1), STRIPS, send_before, 0)
+
+        @pl.when(gives_first)
+        def _():
+            pltpu.make_async_copy(sp.at[c], ahead, rq).start()
 
     def send_mate(i, _):
         strip = (c + i) % STRIPS
@@ -266,11 +291,6 @@
         rd[k] = state[k]
 
     entry = jnp.where(z == 0, rx[0] - rx[0], zero)
-    local_last = entry
-    for k in range(0, 8, 2):
-        local_last = coarse_two(cf, local_last, rd[k], rd[k + 1])[1]
-    pack_halves(local_last, pk)
-
     def send_main(packed, plane, slot, sem):
         pltpu.make_async_remote_copy(
             packed, lr.at[slot, pl.ds(1, 2)], s2.at[sem], r2.at[slot], at(plane, c), pl.DeviceIdType.MESH
@@ -286,83 +306,124 @@
         send_main(packed, plane, slot, sem)
         send_sides(packed, plane, slot, sem)
 
+    def send_window(window, plane, slot, sem):
+        pltpu.make_async_remote_copy(
+            window, ul.at[slot], s2.at[sem], r4.at[slot], at(plane, c), pl.DeviceIdType.MESH
+        ).start()
+
+    def window_arrived(slot):
+        pltpu.make_async_copy(ul.at[slot], ul.at[slot], r4.at[slot]).wait()
+
     def arrived(slot):
         pltpu.make_async_copy(lr.at[slot], lr.at[slot], r2.at[slot]).wait()
         return unpack_window([lr[slot, h] for h in range(4)])
 
+    lane64 = lane_ids(64)
+
+    def chain(err):
+        for xx in range(NX_DEV):
+            first = rx[2 * xx] + err
+            mid, err = coarse_two(cf, err, rd[2 * xx], rd[2 * xx + 1])
+            second = rx[2 * xx + 1] + mid
+            po[xx] = jnp.where(lane64 < 64, pltpu.roll(first, 96, 1), pltpu.roll(second, 32, 1))
+        return err
+
+    def send_out(i, _):
+        xx, ss = (x + i // NS) % NX_DEV, (s + i) % NS
+        pltpu.make_async_remote_copy(
+            po.at[xx, pl.ds(8 * ss, 8)], ob.at[c], s3, r3, (z * NX_DEV + xx, ss), pl.DeviceIdType.MESH
+        ).start()
+        return 0
+
+    def send_results():
+        lax.fori_loop(1, STRIPS, send_out, 0)
+        pltpu.make_async_copy(po.at[x, pl.ds(8 * s, 8)], ob.at[c], r3).start()
+
     @pl.when(z == 0)
     def _():
+        e = chain(entry)
+        lw[0] = e
+        pack_halves(e, pk)
         send_sides(pk, 0, 0, 0)
         pltpu.make_async_copy(pk, lr.at[0, pl.ds(1, 2)], r2.at[0]).start()
-        send_three(pk, 1, 0, 1)
+        pl.semaphore_wait(ready.at[1], 1)
+        send_window(lw.at[0], 1, 0, 1)
+        send_results()
         e = arrived(0)
         for j in range(1, 4):
-            e = coarse_eight(cf, e) + arrived(j)
-            if j == 3:
-                pack_halves(e, pe.at[3])
-                for plane in (7, 6, 5, 4):
-                    send_three(pe.at[3], plane, 0, plane)
-            else:
-                pack_halves(e, pe.at[j])
-        for plane in (3, 2):
-            send_three(pe.at[plane - 1], plane, 0, plane)
-        eb[...] = entry
+            e = coarse_eight(cf, e)
+            window_arrived(j - 1)
+            e = e + ul[j - 1]
+            if j < 3:
+                lw[j] = e
+                pl.semaphore_wait(ready.at[j + 1], 1)
+                send_window(lw.at[j], j + 1, 0, j + 1)
+        pack_halves(e, pe)
+        for plane in (7, 6, 5, 4):
+            pl.semaphore_wait(ready.at[plane], 3)
+            send_three(pe, plane, 0, plane)
+
+    @pl.when(z > 0)
+    def _():
+        local_last = zero
+        for k in range(0, 8, 2):
+            local_last = coarse_two(cf, local_last, rd[k], rd[k + 1])[1]
+        lw[0] = local_last
 
     @pl.when(jnp.logical_and(z >= 1, z <= 3))
     def _():
-        send_three(pk, 0, z, 1)
+        send_window(lw.at[0], 0, z - 1, 1)
+
+    @pl.when(z == 4)
+    def _():
+        pack_halves(lw[0], pk)
+        send_three(pk, 7, 1, 7)
 
     for plane in (7, 6, 5):
 
-        @pl.when(jnp.logical_and(z >= 4, z < plane))
+        @pl.when(jnp.logical_and(z >= (5 if plane == 7 else 4), z < plane))
         def _(plane=plane):
-            send_three(pk, plane, z - 3, plane)
+            send_window(lw.at[0], plane, z - 4, plane)
 
     for j in range(4, 7):
 
-        @pl.when(z > j)
+        @pl.when(jnp.logical_and(z > j, z < 7) if j == 4 else z > j)
         def _(j=j):
-            ul[j - 4] = arrived(j - 3)
-
-    @pl.when(z >= 1)
-    def _():
-        eb[...] = lax.fori_loop(0, jnp.maximum(z - 4, 0), lambda j, e: coarse_eight(cf, e) + ul[j], arrived(0))
-
-    lane64 = lane_ids(64)
-    err = eb[...]
-    for xx in range(NX_DEV):
-        first = rx[2 * xx] + err
-        mid, err = coarse_two(cf, err, rd[2 * xx], rd[2 * xx + 1])
-        second = rx[2 * xx + 1] + mid
-        po[xx] = jnp.where(lane64 < 64, pltpu.roll(first, 96, 1), pltpu.roll(second, 32, 1))
-
-        def send_out(i, _, xx=xx):
-            ss = (s + i) % NS
-            rows = po.at[xx, pl.ds(8 * ss, 8)]
-            own = jnp.logical_and(xx == x, i == 0)
-
-            @pl.when(own)
-            def _():
-                pltpu.make_async_copy(rows, ob.at[c], r3).start()
-
-            @pl.when(jnp.logical_not(own))
-            def _():
-                pltpu.make_async_remote_copy(
-                    rows, ob.at[c], s3, r3, (z * NX_DEV + xx, ss), pl.DeviceIdType.MESH
-                ).start()
-
-            return 0
-
-        lax.fori_loop(0, NS, send_out, 0)
+            window_arrived(j - 4)
+
+    @pl.when(z == 7)
+    def _():
+        ul[0] = arrived(1)
+
+    @pl.when(jnp.logical_and(z >= 1, z <= 3))
+    def _():
+        window_arrived(0)
+        e_in[...] = ul[0]
+
+    @pl.when(z >= 4)
+    def _():
+        e_in[...] = lax.fori_loop(
+            0, jnp.maximum(z - 4, 0), lambda j, e: coarse_eight(cf, e) + ul[j], arrived(0)
+        )
+
+    @pl.when(z > 0)
+    def _():
+        chain(e_in[...])
+        send_results()
 
     pltpu.make_async_copy(ob, ob, r3).wait()
 
     sent = sb.at[pl.ds(0, STRIPS - 1)]
     pltpu.make_async_copy(sent, sent, s1).wait()
 
-    @pl.when(last_x)
+    @pl.when(gives_next)
     def _():
         pltpu.make_async_copy(sp, sp, sq).wait()
+
+    @pl.when(gives_first)
+    def _():
+        most = sp.at[pl.ds(0, STRIPS - 1)]
+        pltpu.make_async_copy(most, most, sq).wait()
 
     @pl.when(z == 0)
     def _():
@@ -414,11 +475,12 @@
             f32((20, 64, LANES)),
             f32((8, 64, LANES)),
             f32((8, 64, LANES)),
+            f32((2, 16, LANES)),
+            f32((2, 16, LANES)),
+            f32((2, 4, 16, LANES)),
+            f32((3, 64, LANES)),
+            f32((3, 64, LANES)),
             f32((64, LANES)),
-            f32((2, 16, LANES)),
-            f32((4, 2, 16, LANES)),
-            f32((4, 4, 16, LANES)),
-            f32((3, 64, LANES)),
             f32((NX_DEV, 64, LANES)),
             sem((4,)),
             sem,
@@ -426,9 +488,11 @@
             sem,
             sem,
             sem((8,)),
-            sem((4,)),
+            sem((2,)),
+            sem((3,)),
             sem,
             sem,
+            pltpu.SemaphoreType.REGULAR((NZ,)),
         ],
         compiler_params=pltpu.CompilerParams(
             collective_id=0, has_side_effects=True, vmem_limit_bytes=56 * 1024 * 1024

time: 36.2 us -> 34.1 us (0.942)
  the two profiles are of different devices: /device:TPU:65 before, /device:TPU:161 now
where the time goes in v3:
time: 34.1 us; the launch traced here: 34 us
  Pallas kernels  34 us (100%)
    pallas_call x1, Pallas kernels, per_device(): pl.pallas_call(kernel, out_shape=jax.ShapeDtypeStruct((STRIPS, 8, LANES),...  32.3 us
    pallas_call x1, Pallas kernels, per_device(): pl.pallas_call(place_rows, out_shape=jax.ShapeDtypeStruct((2, 8, 2048), j...  1.66 us

profile of v3, /device:TPU:161, one launch (start us, length us, event | category | flops | bytes accessed | tf_op | source)
XLA Modules:
  0.0 34.0 jit_solution(17431839840111696850)
XLA Ops:
  0.0 32.3 %cycle.1.ob = f32[32,8,128]{2,1,0:T(8,128)} custom-call(f32[8,2048]{1,0:T(8,128)} %initial.1, f32[8,2048]{1,0:T(8,128)} %source.1, f32[8,2048]{1,0:T(8,128)} %rate.1, f32[8,2048]{1,0:T(8,128)} %velx.1, f32[8,2048]{1,0:T(8,128)} %vely.1, f32[8]{0:T(128)} %strengths.1, f32[2,8,2048]{2,1,0:T(8,128)} %guess.1), custom_call_target="tpu_custom_call" | custom-call | flops 20000000 | bytes 700000 | tf_op jit(solution)/shard_map/cycle/pallas_call | solution.py:461
  32.3 1.7 %place.1 = f32[2,8,2048]{2,1,0:T(8,128)} custom-call(f32[32,8,128]{2,1,0:T(8,128)} %cycle.1.ob), custom_call_target="tpu_custom_call" | custom-call | tf_op jit(solution)/shard_map/place/pallas_call | solution.py:504

commit v4 on v3

--- a/solution.py
+++ b/solution.py
@@ -13,6 +13,12 @@
 NS = 8
 STRIPS = 32
 LANES = 128
+
+
+OFFSETS = sorted(
+    ((dx, dy, dc) for dx in range(4) for dy in range(4) for dc in range(2)),
+    key=lambda o: (-min(o[0], 4 - o[0]) - min(o[1], 4 - o[1]), -o[2]),
+)
 
 
 def place_of(strip):
@@ -115,11 +121,13 @@
     def greet(device):
         pl.semaphore_signal(barrier, inc=1, device_id=device, device_id_type=pl.DeviceIdType.MESH)
 
-    def greet_mate(i, _):
-        greet(at(z, (c + i) % STRIPS))
-        return 0
-
-    lax.fori_loop(1, STRIPS, greet_mate, 0)
+    def mate(dx, dy, dc):
+        ps = (s + 2 * dy) % NS
+        return (x + dx) % NX_DEV, ps if dc == 0 else ps + 1 - 2 * (s % 2)
+
+    for offset in OFFSETS[:-1]:
+        px, ps = mate(*offset)
+        greet((z * NX_DEV + px, ps))
 
     def greet_before(i, _):
         greet(((z - 1) * NX_DEV + NX_DEV - 1, i))
@@ -231,27 +239,28 @@
     def _():
         to = jnp.where(gives_next, z + 1, 0)
 
-        def send_before(i, _):
-            strip = (c + i) % STRIPS
+        def give(offset):
+            px, ps = mate(*offset)
             pltpu.make_async_remote_copy(
-                sp.at[strip], ahead, sq, rq, at(to, strip), pl.DeviceIdType.MESH
+                sp.at[strip_of(px, ps)], ahead, sq, rq, (to * NX_DEV + px, ps), pl.DeviceIdType.MESH
             ).start()
-            return 0
-
-        lax.fori_loop(jnp.where(gives_next, 0, 1), STRIPS, send_before, 0)
+
+        for offset in OFFSETS[:-1]:
+            give(offset)
+
+        @pl.when(gives_next)
+        def _():
+            give(OFFSETS[-1])
 
         @pl.when(gives_first)
         def _():
             pltpu.make_async_copy(sp.at[c], ahead, rq).start()
 
-    def send_mate(i, _):
-        strip = (c + i) % STRIPS
+    for offset in OFFSETS[:-1]:
+        px, ps = mate(*offset)
         pltpu.make_async_remote_copy(
-            sb.at[strip], mine, s1, r1, at(z, strip), pl.DeviceIdType.MESH
+            sb.at[strip_of(px, ps)], mine, s1, r1, (z * NX_DEV + px, ps), pl.DeviceIdType.MESH
         ).start()
-        return 0
-
-    lax.fori_loop(1, STRIPS, send_mate, 0)
     pltpu.make_async_copy(sb.at[c], mine, r1).start()
     pltpu.make_async_copy(rb, rb, r1).wait()
 
@@ -328,15 +337,12 @@
             po[xx] = jnp.where(lane64 < 64, pltpu.roll(first, 96, 1), pltpu.roll(second, 32, 1))
         return err
 
-    def send_out(i, _):
-        xx, ss = (x + i // NS) % NX_DEV, (s + i) % NS
-        pltpu.make_async_remote_copy(
-            po.at[xx, pl.ds(8 * ss, 8)], ob.at[c], s3, r3, (z * NX_DEV + xx, ss), pl.DeviceIdType.MESH
-        ).start()
-        return 0
-
     def send_results():
-        lax.fori_loop(1, STRIPS, send_out, 0)
+        for offset in OFFSETS[:-1]:
+            px, ps = mate(*offset)
+            pltpu.make_async_remote_copy(
+                po.at[px, pl.ds(8 * ps, 8)], ob.at[c], s3, r3, (z * NX_DEV + px, ps), pl.DeviceIdType.MESH
+            ).start()
         pltpu.make_async_copy(po.at[x, pl.ds(8 * s, 8)], ob.at[c], r3).start()
 
     @pl.when(z == 0)

time: 34.1 us -> 32.9 us (0.965)
  Pallas kernels: 34 us -> 32.6 us
    pallas_call x1, Pallas kernels: 32.3 us -> 30.9 us  [per_device(): pl.pallas_call(kernel, out_shape=jax.ShapeDtypeStruct((STRIPS, 8, LANES),...]
where the time goes in v4:
time: 32.9 us; the launch traced here: 32.6 us
  Pallas kernels  32.6 us (99%)
    pallas_call x1, Pallas kernels, per_device(): pl.pallas_call(kernel, out_shape=jax.ShapeDtypeStruct((STRIPS, 8, LANES),...  30.9 us
    pallas_call x1, Pallas kernels, per_device(): pl.pallas_call(place_rows, out_shape=jax.ShapeDtypeStruct((2, 8, 2048), j...  1.66 us

profile of v4, /device:TPU:161, one launch (start us, length us, event | category | flops | bytes accessed | tf_op | source)
XLA Modules:
  0.0 32.6 jit_solution(4976270659094221435)
XLA Ops:
  0.0 30.9 %cycle.1.ob = f32[32,8,128]{2,1,0:T(8,128)} custom-call(f32[8,2048]{1,0:T(8,128)} %initial.1, f32[8,2048]{1,0:T(8,128)} %source.1, f32[8,2048]{1,0:T(8,128)} %rate.1, f32[8,2048]{1,0:T(8,128)} %velx.1, f32[8,2048]{1,0:T(8,128)} %vely.1, f32[8]{0:T(128)} %strengths.1, f32[2,8,2048]{2,1,0:T(8,128)} %guess.1), custom_call_target="tpu_custom_call" | custom-call | flops 20000000 | bytes 700000 | tf_op jit(solution)/shard_map/cycle/pallas_call | solution.py:467
  30.9 1.7 %place.1 = f32[2,8,2048]{2,1,0:T(8,128)} custom-call(f32[32,8,128]{2,1,0:T(8,128)} %cycle.1.ob), custom_call_target="tpu_custom_call" | custom-call | tf_op jit(solution)/shard_map/place/pallas_call | solution.py:510

commit v5 on v4

--- a/solution.py
+++ b/solution.py
@@ -101,8 +101,8 @@
 
 def kernel(
     initial, source, rate, velx, vely, strengths, guess, ob,
-    amp, gb, fb, ib, sb, sp, rb, pb, cf, rx, rd, pk, pe, lr, ul, lw, e_in, po,
-    ld, s1, r1, sq, rq, s2, r2, r4, s3, r3, ready,
+    amp, gb, fb, ib, sb, sf, sp, rb, rp, pb, cf, rx, rd, pk, pe, lr, ul, lw, e_in, po,
+    ld, s1, r1, s0, r0, sq, rq, s2, r2, r4, s3, r3, ready,
 ):
     t, s = lax.axis_index("tm"), lax.axis_index("space")
     z, x = t // NX_DEV, t % NX_DEV
@@ -162,11 +162,12 @@
     load_guess.start()
     load_amp = pltpu.make_async_copy(strengths, amp, ld.at[3])
     load_amp.start()
-    for which, field in enumerate((rate, velx, vely, source)):
-
-        @pl.when(x == which)
-        def _(field=field):
-            pltpu.make_async_copy(field, fb, ld.at[1]).start()
+    load_fields = [
+        pltpu.make_async_copy(field, fb.at[which], ld.at[4 + which])
+        for which, field in enumerate((rate, velx, vely, source))
+    ]
+    for load in load_fields:
+        load.start()
 
     @pl.when(gives_first)
     def _():
@@ -178,7 +179,6 @@
 
     load_guess.wait()
     load_amp.wait()
-    pltpu.make_async_copy(rate, fb, ld.at[1]).wait()
 
     lane8 = lane_ids(8)
 
@@ -199,10 +199,21 @@
 
         windows(lambda k, i=i: gb[i, :, LANES * k : LANES * (k + 1)], put_guess)
 
-    def put_field(strip, value):
-        sb[strip, 2] = value
-
-    windows(lambda k: fb[:, LANES * k : LANES * (k + 1)], put_field)
+    for load in load_fields:
+        load.wait()
+    for y in range(4):
+        k = 4 * y + (x if y % 2 == 0 else 3 - x)
+        before, here, after = (
+            pl.ds(pl.multiple_of(LANES * ((k + move) % 16), LANES), LANES) for move in (15, 0, 1)
+        )
+        for f in range(4):
+            tile = fb[f, :, here]
+            sf[2 * y, f] = jnp.where(
+                lane8 < 32, pltpu.roll(fb[f, :, before], 32, 1), pltpu.roll(tile, 32, 1)
+            )
+            sf[2 * y + 1, f] = jnp.where(
+                lane8 < 96, pltpu.roll(tile, 96, 1), pltpu.roll(fb[f, :, after], 96, 1)
+            )
 
     @pl.when(gives)
     def _():
@@ -231,7 +242,8 @@
         signal_ready(c_lo)
         signal_ready(c_hi)
 
-    mine = rb.at[pl.ds(3 * x, 3), pl.ds(8 * s, 8)]
+    mine = rb.at[pl.ds(2 * x, 2), pl.ds(8 * s, 8)]
+    mine_fields = rp.at[:, pl.ds(8 * s, 8)]
 
     ahead = pb.at[pl.ds(8 * s, 8)]
 
@@ -256,15 +268,22 @@
         def _():
             pltpu.make_async_copy(sp.at[c], ahead, rq).start()
 
+    for offset in OFFSETS[:-1]:
+        px, ps = mate(*offset)
+        if offset[0] == 0:
+            pltpu.make_async_remote_copy(
+                sf.at[ps], mine_fields, s0, r0, (z * NX_DEV + px, ps), pl.DeviceIdType.MESH
+            ).start()
     for offset in OFFSETS[:-1]:
         px, ps = mate(*offset)
         pltpu.make_async_remote_copy(
             sb.at[strip_of(px, ps)], mine, s1, r1, (z * NX_DEV + px, ps), pl.DeviceIdType.MESH
         ).start()
     pltpu.make_async_copy(sb.at[c], mine, r1).start()
-    pltpu.make_async_copy(rb, rb, r1).wait()
-
-    d, a, b = rb[2], rb[5], rb[8]
+    pltpu.make_async_copy(sf.at[s], mine_fields, r0).start()
+    pltpu.make_async_copy(rp, rp, r0).wait()
+
+    d, a, b = rp[0], rp[1], rp[2]
     row = lax.broadcasted_iota(jnp.int32, (64, LANES), 0)
     col = lax.broadcasted_iota(jnp.int32, (64, LANES), 1) + (64 * c - 32)
     zero = jnp.zeros((64, LANES), jnp.float32)
@@ -280,14 +299,15 @@
         cf[10 + k] = lanes(cf[5 + k], 1)
         cf[15 + k] = lanes(cf[5 + k], -1)
 
+    pltpu.make_async_copy(rb, rb, r1).wait()
     pltpu.make_async_copy(pb, pb, rq).wait()
 
     def forced(u, tile, m):
         strength = jnp.broadcast_to(rb[tile, 0:8, m : m + 1], (8, LANES))
-        push = rb[11].reshape(8, 8, LANES) * strength[None]
+        push = rp[3].reshape(8, 8, LANES) * strength[None]
         return stencil(cf, 0, u) + push.reshape(64, LANES)
 
-    tiles = [3 * (k // 2) + k % 2 for k in range(8)]
+    tiles = list(range(8))
     state = [pb[...]] + [rb[tile] for tile in tiles[:-1]]
     for m in range(M):
         state = [forced(u, tile, m) for u, tile in zip(state, tiles)]
@@ -421,6 +441,8 @@
 
     sent = sb.at[pl.ds(0, STRIPS - 1)]
     pltpu.make_async_copy(sent, sent, s1).wait()
+    sent_fields = sf.at[pl.ds(0, NS - 1)]
+    pltpu.make_async_copy(sent_fields, sent_fields, s0).wait()
 
     @pl.when(gives_next)
     def _():
@@ -472,11 +494,13 @@
         scratch_shapes=[
             pltpu.SMEM((8,), jnp.float32),
             f32((2, 8, 2048)),
+            f32((4, 8, 2048)),
             f32((8, 2048)),
-            f32((8, 2048)),
-            f32((STRIPS, 3, 8, LANES)),
+            f32((STRIPS, 2, 8, LANES)),
+            f32((NS, 4, 8, LANES)),
             f32((STRIPS, 8, LANES)),
-            f32((12, 64, LANES)),
+            f32((8, 64, LANES)),
+            f32((4, 64, LANES)),
             f32((64, LANES)),
             f32((20, 64, LANES)),
             f32((8, 64, LANES)),
@@ -488,7 +512,9 @@
             f32((3, 64, LANES)),
             f32((64, LANES)),
             f32((NX_DEV, 64, LANES)),
-            sem((4,)),
+            sem((8,)),
+            sem,
+            sem,
             sem,
             sem,
             sem,

time: 32.9 us -> 31.5 us (0.957)
  Pallas kernels: 32.6 us -> 31.2 us
    pallas_call x1, Pallas kernels: 30.9 us -> 29.5 us  [per_device(): pl.pallas_call(kernel, out_shape=jax.ShapeDtypeStruct((STRIPS, 8, LANES),...]
where the time goes in v5:
time: 31.5 us; the launch traced here: 31.2 us
  Pallas kernels  31.2 us (99%)
    pallas_call x1, Pallas kernels, per_device(): pl.pallas_call(kernel, out_shape=jax.ShapeDtypeStruct((STRIPS, 8, LANES),...  29.5 us
    pallas_call x1, Pallas kernels, per_device(): pl.pallas_call(place_rows, out_shape=jax.ShapeDtypeStruct((2, 8, 2048), j...  1.66 us

profile of v5, /device:TPU:161, one launch (start us, length us, event | category | flops | bytes accessed | tf_op | source)
XLA Modules:
  0.0 31.2 jit_solution(10801806237536971652)
XLA Ops:
  0.0 29.5 %cycle.1.ob = f32[32,8,128]{2,1,0:T(8,128)} custom-call(f32[8,2048]{1,0:T(8,128)} %initial.1, f32[8,2048]{1,0:T(8,128)} %source.1, f32[8,2048]{1,0:T(8,128)} %rate.1, f32[8,2048]{1,0:T(8,128)} %velx.1, f32[8,2048]{1,0:T(8,128)} %vely.1, f32[8]{0:T(128)} %strengths.1, f32[2,8,2048]{2,1,0:T(8,128)} %guess.1), custom_call_target="tpu_custom_call" | custom-call | flops 20000000 | bytes 700000 | tf_op jit(solution)/shard_map/cycle/pallas_call | solution.py:489
  29.5 1.7 %place.1 = f32[2,8,2048]{2,1,0:T(8,128)} custom-call(f32[32,8,128]{2,1,0:T(8,128)} %cycle.1.ob), custom_call_target="tpu_custom_call" | custom-call | tf_op jit(solution)/shard_map/place/pallas_call | solution.py:536

commit v6 on v5

--- a/solution.py
+++ b/solution.py
@@ -21,16 +21,24 @@
 )
 
 
+def div(a, b):
+    return lax.div(a, jnp.int32(b))
+
+
+def rem(a, b):
+    return lax.rem(a, jnp.int32(b))
+
+
 def place_of(strip):
-    chip, core = strip // 2, strip % 2
-    y, q = chip // 4, chip % 4
-    x = q + (y % 2) * (3 - 2 * q)
+    chip, core = div(strip, 2), rem(strip, 2)
+    y, q = div(chip, 4), rem(chip, 4)
+    x = q + rem(y, 2) * (3 - 2 * q)
     return x, 2 * y + core
 
 
 def strip_of(x, s):
-    y, core = s // 2, s % 2
-    q = x + (y % 2) * (3 - 2 * x)
+    y, core = div(s, 2), rem(s, 2)
+    q = x + rem(y, 2) * (3 - 2 * x)
     return 2 * (4 * y + q) + core
 
 
@@ -101,32 +109,32 @@
 
 def kernel(
     initial, source, rate, velx, vely, strengths, guess, ob,
-    amp, gb, fb, ib, sb, sf, sp, rb, rp, pb, cf, rx, rd, pk, pe, lr, ul, lw, e_in, po,
+    amp, gb, fb, ib, sb, sf, sp, rb, rp, pb, cf, rx, rd, pk, pe, lr, ul, lw, e_in, ahead_3, po,
     ld, s1, r1, s0, r0, sq, rq, s2, r2, r4, s3, r3, ready,
 ):
     t, s = lax.axis_index("tm"), lax.axis_index("space")
-    z, x = t // NX_DEV, t % NX_DEV
+    z, x = div(t, NX_DEV), rem(t, NX_DEV)
     c = strip_of(x, s)
-    c_lo, c_hi = (c + STRIPS - 1) % STRIPS, (c + 1) % STRIPS
+    lo, here, hi = place_of(rem(c + STRIPS - 1, STRIPS)), (x, s), place_of(rem(c + 1, STRIPS))
+    xs = [rem(x + dx, NX_DEV) for dx in range(NX_DEV)]
+    other = 1 - 2 * rem(s, 2)
+    ss = [rem(s + 2 * dy, NS) for dy in range(4)]
+    mates = {(dx, dy, dc): (xs[dx], ss[dy] + other * dc) for dx, dy, dc in OFFSETS}
+
     gives_next = jnp.logical_and(x == NX_DEV - 1, z < NZ - 1)
     gives_first = jnp.logical_and(x == 0, z == 0)
     gives = jnp.logical_or(gives_next, gives_first)
 
-    def at(plane, strip):
-        px, ps = place_of(strip)
-        return (plane * NX_DEV + px, ps)
+    def at(plane, place):
+        return (plane * NX_DEV + place[0], place[1])
 
     barrier = pltpu.get_barrier_semaphore()
 
     def greet(device):
         pl.semaphore_signal(barrier, inc=1, device_id=device, device_id_type=pl.DeviceIdType.MESH)
 
-    def mate(dx, dy, dc):
-        ps = (s + 2 * dy) % NS
-        return (x + dx) % NX_DEV, ps if dc == 0 else ps + 1 - 2 * (s % 2)
-
     for offset in OFFSETS[:-1]:
-        px, ps = mate(*offset)
+        px, ps = mates[offset]
         greet((z * NX_DEV + px, ps))
 
     def greet_before(i, _):
@@ -136,27 +144,32 @@
     lax.fori_loop(0, jnp.where(z > 0, NS, 0), greet_before, 0)
 
     def greet_three(plane):
-        greet(at(plane, c_lo))
-        greet(at(plane, c))
-        greet(at(plane, c_hi))
+        greet(at(plane, lo))
+        greet(at(plane, here))
+        greet(at(plane, hi))
 
     @pl.when(z == 0)
     def _():
         for plane in range(1, 4):
-            greet(at(plane, c))
+            greet(at(plane, here))
         for plane in range(4, NZ):
             greet_three(plane)
 
     def greet_upper(plane, _):
-        greet(at(plane, c))
+        greet(at(plane, here))
         return 0
 
-    lax.fori_loop(4, jnp.maximum(z, 4), greet_upper, 0)
+    first_upper = jnp.where(z == 7, 4, 3)
+    lax.fori_loop(first_upper, jnp.maximum(z, first_upper), greet_upper, 0)
+
+    @pl.when(z >= 6)
+    def _():
+        greet(at(z - 3, lo))
+        greet(at(z - 3, hi))
 
     @pl.when(z == 7)
     def _():
-        greet(at(4, c_lo))
-        greet(at(4, c_hi))
+        greet_three(3)
 
     load_guess = pltpu.make_async_copy(guess, gb, ld.at[0])
     load_guess.start()
@@ -203,16 +216,16 @@
         load.wait()
     for y in range(4):
         k = 4 * y + (x if y % 2 == 0 else 3 - x)
-        before, here, after = (
+        k_lo, k_at, k_hi = (
             pl.ds(pl.multiple_of(LANES * ((k + move) % 16), LANES), LANES) for move in (15, 0, 1)
         )
         for f in range(4):
-            tile = fb[f, :, here]
+            tile = fb[f, :, k_at]
             sf[2 * y, f] = jnp.where(
-                lane8 < 32, pltpu.roll(fb[f, :, before], 32, 1), pltpu.roll(tile, 32, 1)
+                lane8 < 32, pltpu.roll(fb[f, :, k_lo], 32, 1), pltpu.roll(tile, 32, 1)
             )
             sf[2 * y + 1, f] = jnp.where(
-                lane8 < 96, pltpu.roll(tile, 96, 1), pltpu.roll(fb[f, :, after], 96, 1)
+                lane8 < 96, pltpu.roll(tile, 96, 1), pltpu.roll(fb[f, :, k_hi], 96, 1)
             )
 
     @pl.when(gives)
@@ -225,22 +238,22 @@
         windows(lambda k: ib[:, LANES * k : LANES * (k + 1)], put_before)
 
     hubs = jnp.where(z == 0, 0, jnp.where(z < 4, 1, 3))
-    uppers = jnp.where(z == 4, 5, jnp.where(z == 5, 2, jnp.where(z == 6, 1, 0)))
+    uppers = jnp.where(z == 3, 8, jnp.where(z == 4, 5, jnp.where(z == 5, 2, jnp.where(z == 6, 1, 0))))
     pl.semaphore_wait(barrier, STRIPS - 1 + jnp.where(gives_next, STRIPS, 0) + hubs + uppers)
 
-    def signal_ready(strip):
+    def signal_ready(place):
         pl.semaphore_signal(
-            ready.at[z], inc=1, device_id=at(0, strip), device_id_type=pl.DeviceIdType.MESH
+            ready.at[z], inc=1, device_id=at(0, place), device_id_type=pl.DeviceIdType.MESH
         )
 
     @pl.when(z > 0)
     def _():
-        signal_ready(c)
+        signal_ready(here)
 
     @pl.when(z >= 4)
     def _():
-        signal_ready(c_lo)
-        signal_ready(c_hi)
+        signal_ready(lo)
+        signal_ready(hi)
 
     mine = rb.at[pl.ds(2 * x, 2), pl.ds(8 * s, 8)]
     mine_fields = rp.at[:, pl.ds(8 * s, 8)]
@@ -252,7 +265,7 @@
         to = jnp.where(gives_next, z + 1, 0)
 
         def give(offset):
-            px, ps = mate(*offset)
+            px, ps = mates[offset]
             pltpu.make_async_remote_copy(
                 sp.at[strip_of(px, ps)], ahead, sq, rq, (to * NX_DEV + px, ps), pl.DeviceIdType.MESH
             ).start()
@@ -269,13 +282,13 @@
             pltpu.make_async_copy(sp.at[c], ahead, rq).start()
 
     for offset in OFFSETS[:-1]:
-        px, ps = mate(*offset)
+        px, ps = mates[offset]
         if offset[0] == 0:
             pltpu.make_async_remote_copy(
                 sf.at[ps], mine_fields, s0, r0, (z * NX_DEV + px, ps), pl.DeviceIdType.MESH
             ).start()
     for offset in OFFSETS[:-1]:
-        px, ps = mate(*offset)
+        px, ps = mates[offset]
         pltpu.make_async_remote_copy(
             sb.at[strip_of(px, ps)], mine, s1, r1, (z * NX_DEV + px, ps), pl.DeviceIdType.MESH
         ).start()
@@ -322,13 +335,13 @@
     entry = jnp.where(z == 0, rx[0] - rx[0], zero)
     def send_main(packed, plane, slot, sem):
         pltpu.make_async_remote_copy(
-            packed, lr.at[slot, pl.ds(1, 2)], s2.at[sem], r2.at[slot], at(plane, c), pl.DeviceIdType.MESH
+            packed, lr.at[slot, pl.ds(1, 2)], s2.at[sem], r2.at[slot], at(plane, here), pl.DeviceIdType.MESH
         ).start()
 
     def send_sides(packed, plane, slot, sem):
-        for src, part, strip in ((packed.at[0], 3, c_lo), (packed.at[1], 0, c_hi)):
+        for src, part, side in ((packed.at[0], 3, lo), (packed.at[1], 0, hi)):
             pltpu.make_async_remote_copy(
-                src, lr.at[slot, part], s2.at[sem], r2.at[slot], at(plane, strip), pl.DeviceIdType.MESH
+                src, lr.at[slot, part], s2.at[sem], r2.at[slot], at(plane, side), pl.DeviceIdType.MESH
             ).start()
 
     def send_three(packed, plane, slot, sem):
@@ -337,7 +350,7 @@
 
     def send_window(window, plane, slot, sem):
         pltpu.make_async_remote_copy(
-            window, ul.at[slot], s2.at[sem], r4.at[slot], at(plane, c), pl.DeviceIdType.MESH
+            window, ul.at[slot], s2.at[sem], r4.at[slot], at(plane, here), pl.DeviceIdType.MESH
         ).start()
 
     def window_arrived(slot):
@@ -349,45 +362,61 @@
 
     lane64 = lane_ids(64)
 
-    def chain(err):
+    def send_results(xx):
+        for offset in OFFSETS:
+            if offset[0] == 0 and offset != OFFSETS[-1]:
+                ps = mates[offset][1]
+                pltpu.make_async_remote_copy(
+                    po.at[xx, pl.ds(8 * ps, 8)], ob.at[c], s3, r3, (z * NX_DEV + xx, ps), pl.DeviceIdType.MESH
+                ).start()
+        mine_out = po.at[xx, pl.ds(8 * s, 8)]
+
+        @pl.when(x == xx)
+        def _():
+            pltpu.make_async_copy(mine_out, ob.at[c], r3).start()
+
+        @pl.when(x != xx)
+        def _():
+            pltpu.make_async_remote_copy(
+                mine_out, ob.at[c], s3, r3, (z * NX_DEV + xx, s), pl.DeviceIdType.MESH
+            ).start()
+
+    def chain(err, ready_made):
         for xx in range(NX_DEV):
             first = rx[2 * xx] + err
             mid, err = coarse_two(cf, err, rd[2 * xx], rd[2 * xx + 1])
             second = rx[2 * xx + 1] + mid
             po[xx] = jnp.where(lane64 < 64, pltpu.roll(first, 96, 1), pltpu.roll(second, 32, 1))
+            ready_made(xx)
         return err
 
-    def send_results():
-        for offset in OFFSETS[:-1]:
-            px, ps = mate(*offset)
-            pltpu.make_async_remote_copy(
-                po.at[px, pl.ds(8 * ps, 8)], ob.at[c], s3, r3, (z * NX_DEV + px, ps), pl.DeviceIdType.MESH
-            ).start()
-        pltpu.make_async_copy(po.at[x, pl.ds(8 * s, 8)], ob.at[c], r3).start()
-
     @pl.when(z == 0)
     def _():
-        e = chain(entry)
+        def pass_on(e, which, planes):
+            pack_halves(e, pe.at[which])
+            for plane in planes:
+                pl.semaphore_wait(ready.at[plane], 3)
+                send_three(pe.at[which], plane, 0, plane)
+
+        e = chain(entry, lambda xx: None)
         lw[0] = e
         pack_halves(e, pk)
         send_sides(pk, 0, 0, 0)
         pltpu.make_async_copy(pk, lr.at[0, pl.ds(1, 2)], r2.at[0]).start()
         pl.semaphore_wait(ready.at[1], 1)
         send_window(lw.at[0], 1, 0, 1)
-        send_results()
+        for xx in range(NX_DEV):
+            send_results(xx)
         e = arrived(0)
-        for j in range(1, 4):
+        for j in range(1, 3):
             e = coarse_eight(cf, e)
             window_arrived(j - 1)
             e = e + ul[j - 1]
-            if j < 3:
-                lw[j] = e
-                pl.semaphore_wait(ready.at[j + 1], 1)
-                send_window(lw.at[j], j + 1, 0, j + 1)
-        pack_halves(e, pe)
-        for plane in (7, 6, 5, 4):
-            pl.semaphore_wait(ready.at[plane], 3)
-            send_three(pe, plane, 0, plane)
+            lw[j] = e
+            pl.semaphore_wait(ready.at[j + 1], 1)
+            send_window(lw.at[j], j + 1, 0, j + 1)
+        pass_on(e, 0, (6, 5, 4))
+        pass_on(coarse_eight(cf, e), 1, (7,))
 
     @pl.when(z > 0)
     def _():
@@ -396,30 +425,44 @@
             local_last = coarse_two(cf, local_last, rd[k], rd[k + 1])[1]
         lw[0] = local_last
 
-    @pl.when(jnp.logical_and(z >= 1, z <= 3))
+    @pl.when(jnp.logical_and(z >= 1, z <= 2))
     def _():
         send_window(lw.at[0], 0, z - 1, 1)
 
-    @pl.when(z == 4)
+    @pl.when(jnp.logical_or(z == 3, z == 4))
     def _():
         pack_halves(lw[0], pk)
-        send_three(pk, 7, 1, 7)
-
-    for plane in (7, 6, 5):
-
-        @pl.when(jnp.logical_and(z >= (5 if plane == 7 else 4), z < plane))
+
+    @pl.when(z == 3)
+    def _():
+        send_three(pk, 7, 2, 7)
+
+    for plane in (7, 6, 5, 4):
+        if plane >= 6:
+
+            @pl.when(z == plane - 3)
+            def _(plane=plane):
+                send_three(pk, plane, 1, plane)
+
+        @pl.when(jnp.logical_and(z >= (3 if plane < 6 else plane - 2), z < plane))
         def _(plane=plane):
-            send_window(lw.at[0], plane, z - 4, plane)
-
-    for j in range(4, 7):
-
-        @pl.when(jnp.logical_and(z > j, z < 7) if j == 4 else z > j)
-        def _(j=j):
-            window_arrived(j - 4)
+            send_window(lw.at[0], plane, z - (4 if plane == 7 else 3), plane)
+
+    for slot in range(3):
+
+        @pl.when((z == 4) | (z == 5) if slot == 0 else z >= 4 + slot)
+        def _(slot=slot):
+            window_arrived(slot)
+
+    @pl.when(z >= 6)
+    def _():
+        ul[0] = arrived(1)
+
+    ahead_3[...] = zero
 
     @pl.when(z == 7)
     def _():
-        ul[0] = arrived(1)
+        ahead_3[...] = arrived(2)
 
     @pl.when(jnp.logical_and(z >= 1, z <= 3))
     def _():
@@ -429,13 +472,12 @@
     @pl.when(z >= 4)
     def _():
         e_in[...] = lax.fori_loop(
-            0, jnp.maximum(z - 4, 0), lambda j, e: coarse_eight(cf, e) + ul[j], arrived(0)
+            0, jnp.minimum(z - 3, 3), lambda j, e: coarse_eight(cf, e) + ul[j], arrived(0) + ahead_3[...]
         )
 
     @pl.when(z > 0)
     def _():
-        chain(e_in[...])
-        send_results()
+        chain(e_in[...], send_results)
 
     pltpu.make_async_copy(ob, ob, r3).wait()
 
@@ -459,13 +501,13 @@
         for plane in range(1, NZ):
             pltpu.make_async_copy(lr.at[0], lr.at[0], s2.at[plane]).wait()
 
-    @pl.when(jnp.logical_and(z >= 1, z <= 3))
+    @pl.when(jnp.logical_and(z >= 1, z <= 2))
     def _():
         pltpu.make_async_copy(lr.at[0], lr.at[0], s2.at[1]).wait()
 
-    for plane in (7, 6, 5):
-
-        @pl.when(jnp.logical_and(z >= 4, z < plane))
+    for plane in (7, 6, 5, 4):
+
+        @pl.when(jnp.logical_and(z >= 3, z < plane))
         def _(plane=plane):
             pltpu.make_async_copy(lr.at[0], lr.at[0], s2.at[plane]).wait()
 
@@ -506,11 +548,12 @@
             f32((8, 64, LANES)),
             f32((8, 64, LANES)),
             f32((2, 16, LANES)),
-            f32((2, 16, LANES)),
-            f32((2, 4, 16, LANES)),
+            f32((2, 2, 16, LANES)),
+            f32((3, 4, 16, LANES)),
             f32((3, 64, LANES)),
             f32((3, 64, LANES)),
             f32((64, LANES)),
+            f32((64, LANES)),
             f32((NX_DEV, 64, LANES)),
             sem((8,)),
             sem,
@@ -520,7 +563,7 @@
             sem,
             sem,
             sem((8,)),
-            sem((2,)),
+            sem((3,)),
             sem((3,)),
             sem,
             sem,

time: 31.5 us -> 29.6 us (0.940)
  Pallas kernels: 31.2 us -> 29.5 us
    pallas_call x1, Pallas kernels: 29.5 us -> 27.8 us  [per_device(): pl.pallas_call(kernel, out_shape=jax.ShapeDtypeStruct((STRIPS, 8, LANES),...]
where the time goes in v6:
time: 29.6 us; the launch traced here: 29.5 us
  Pallas kernels  29.5 us (100%)
    pallas_call x1, Pallas kernels, per_device(): pl.pallas_call(kernel, out_shape=jax.ShapeDtypeStruct((STRIPS, 8, LANES),...  27.8 us
    pallas_call x1, Pallas kernels, per_device(): pl.pallas_call(place_rows, out_shape=jax.ShapeDtypeStruct((2, 8, 2048), j...  1.66 us

profile of v6, /device:TPU:161, one launch (start us, length us, event | category | flops | bytes accessed | tf_op | source)
XLA Modules:
  0.0 29.5 jit_solution(6305037324465942057)
XLA Ops:
  0.0 27.8 %cycle.1.ob = f32[32,8,128]{2,1,0:T(8,128)} custom-call(f32[8,2048]{1,0:T(8,128)} %initial.1, f32[8,2048]{1,0:T(8,128)} %source.1, f32[8,2048]{1,0:T(8,128)} %rate.1, f32[8,2048]{1,0:T(8,128)} %velx.1, f32[8,2048]{1,0:T(8,128)} %vely.1, f32[8]{0:T(128)} %strengths.1, f32[2,8,2048]{2,1,0:T(8,128)} %guess.1), custom_call_target="tpu_custom_call" | custom-call | flops 20000000 | bytes 700000 | tf_op jit(solution)/shard_map/cycle/pallas_call | solution.py:531
  27.8 1.7 %place.1 = f32[2,8,2048]{2,1,0:T(8,128)} custom-call(f32[32,8,128]{2,1,0:T(8,128)} %cycle.1.ob), custom_call_target="tpu_custom_call" | custom-call | tf_op jit(solution)/shard_map/place/pallas_call | solution.py:579

commit v7 on v6

--- a/solution.py
+++ b/solution.py
@@ -98,18 +98,44 @@
     return v, w
 
 
-def coarse_eight(cf, u):
-    def body(i, u):
-        for _ in range(2):
-            u = coarse_two(cf, u)[1]
-        return u
-
-    return lax.fori_loop(0, 2, body, u)
+def square_coarse(cf, kf):
+    mid, up, down, left, right = (cf[5 + k] for k in range(5))
+    at_left, at_right = [cf[10 + k] for k in range(5)], [cf[15 + k] for k in range(5)]
+    at_up = [pltpu.roll(cf[5 + k], 1, 0) for k in range(5)]
+    at_down = [pltpu.roll(cf[5 + k], 63, 0) for k in range(5)]
+    kf[0] = (mid * mid + up * at_up[2] + down * at_down[1]) + (left * at_left[4] + right * at_right[3])
+    kf[1] = left * (mid + at_left[0])
+    kf[2] = right * (mid + at_right[0])
+    kf[3] = left * at_left[3]
+    kf[4] = right * at_right[4]
+    kf[5] = pltpu.roll(up * at_up[1], 62, 0)
+    kf[6] = pltpu.roll(down * at_down[2], 2, 0)
+    kf[7] = pltpu.roll(up * (mid + at_up[0]), 63, 0)
+    kf[8] = pltpu.roll(up * at_up[3] + left * at_left[1], 63, 0)
+    kf[9] = pltpu.roll(up * at_up[4] + right * at_right[1], 63, 0)
+    kf[10] = pltpu.roll(down * (mid + at_down[0]), 1, 0)
+    kf[11] = pltpu.roll(down * at_down[3] + left * at_left[2], 1, 0)
+    kf[12] = pltpu.roll(down * at_down[4] + right * at_right[2], 1, 0)
+
+
+def coarse_square(kf, u):
+    left, left2, right, right2 = lanes(u, 1), lanes(u, 2), lanes(u, -1), lanes(u, -2)
+    above = kf[7] * u + (kf[8] * left + kf[9] * right)
+    below = kf[10] * u + (kf[11] * left + kf[12] * right)
+    far = pltpu.roll(kf[5] * u, 2, 0) + pltpu.roll(kf[6] * u, 62, 0)
+    row = (kf[1] * left + kf[2] * right) + (kf[3] * left2 + kf[4] * right2)
+    return (kf[0] * u + far + row) + (pltpu.roll(above, 1, 0) + pltpu.roll(below, 63, 0))
+
+
+def coarse_eight(kf, u):
+    for _ in range(4):
+        u = coarse_square(kf, u)
+    return u
 
 
 def kernel(
     initial, source, rate, velx, vely, strengths, guess, ob,
-    amp, gb, fb, ib, sb, sf, sp, rb, rp, pb, cf, rx, rd, pk, pe, lr, ul, lw, e_in, ahead_3, po,
+    amp, gb, fb, ib, sb, sf, sp, rb, rp, pb, cf, kf, rx, rd, pk, pe, lr, ul, lw, e_in, ahead_3, po,
     ld, s1, r1, s0, r0, sq, rq, s2, r2, r4, s3, r3, ready,
 ):
     t, s = lax.axis_index("tm"), lax.axis_index("space")
@@ -159,17 +185,19 @@
         greet(at(plane, here))
         return 0
 
-    first_upper = jnp.where(z == 7, 4, 3)
-    lax.fori_loop(first_upper, jnp.maximum(z, first_upper), greet_upper, 0)
-
-    @pl.when(z >= 6)
-    def _():
-        greet(at(z - 3, lo))
-        greet(at(z - 3, hi))
+    lax.fori_loop(4, jnp.maximum(z, 4), greet_upper, 0)
 
     @pl.when(z == 7)
     def _():
-        greet_three(3)
+        greet(at(4, lo))
+        greet(at(4, hi))
+
+    @pl.when(z == 3)
+    def _():
+        greet(at(4, here))
+        greet(at(5, here))
+        greet_three(6)
+        greet_three(7)
 
     load_guess = pltpu.make_async_copy(guess, gb, ld.at[0])
     load_guess.start()
@@ -238,12 +266,13 @@
         windows(lambda k: ib[:, LANES * k : LANES * (k + 1)], put_before)
 
     hubs = jnp.where(z == 0, 0, jnp.where(z < 4, 1, 3))
-    uppers = jnp.where(z == 3, 8, jnp.where(z == 4, 5, jnp.where(z == 5, 2, jnp.where(z == 6, 1, 0))))
-    pl.semaphore_wait(barrier, STRIPS - 1 + jnp.where(gives_next, STRIPS, 0) + hubs + uppers)
-
-    def signal_ready(place):
+    uppers = jnp.where(z == 4, 5, jnp.where(z == 5, 2, jnp.where(z == 6, 1, 0)))
+    from_3 = jnp.where(z >= 6, 3, jnp.where(z >= 4, 1, 0))
+    pl.semaphore_wait(barrier, STRIPS - 1 + jnp.where(gives_next, STRIPS, 0) + hubs + uppers + from_3)
+
+    def signal_ready(place, plane=0):
         pl.semaphore_signal(
-            ready.at[z], inc=1, device_id=at(0, place), device_id_type=pl.DeviceIdType.MESH
+            ready.at[z], inc=1, device_id=at(plane, place), device_id_type=pl.DeviceIdType.MESH
         )
 
     @pl.when(z > 0)
@@ -254,6 +283,12 @@
     def _():
         signal_ready(lo)
         signal_ready(hi)
+        signal_ready(here, 3)
+
+    @pl.when(z >= 6)
+    def _():
+        signal_ready(lo, 3)
+        signal_ready(hi, 3)
 
     mine = rb.at[pl.ds(2 * x, 2), pl.ds(8 * s, 8)]
     mine_fields = rp.at[:, pl.ds(8 * s, 8)]
@@ -320,19 +355,30 @@
         push = rp[3].reshape(8, 8, LANES) * strength[None]
         return stencil(cf, 0, u) + push.reshape(64, LANES)
 
-    tiles = list(range(8))
-    state = [pb[...]] + [rb[tile] for tile in tiles[:-1]]
-    for m in range(M):
-        state = [forced(u, tile, m) for u, tile in zip(state, tiles)]
-    for k in range(8):
-        rx[k] = state[k]
-    state = [u - rb[tile] for u, tile in zip(state, tiles)]
-    for m in range(M):
-        state = [stencil(cf, 0, u) for u in state]
-    for k in range(8):
-        rd[k] = state[k]
-
-    entry = jnp.where(z == 0, rx[0] - rx[0], zero)
+    def fine(intervals):
+        state = [pb[...] if k == 0 else rb[k - 1] for k in intervals]
+        for m in range(M):
+            state = [forced(u, k, m) for u, k in zip(state, intervals)]
+        relaxed = state
+        for u, k in zip(relaxed, intervals):
+            rx[k] = u
+        state = [u - rb[k] for u, k in zip(state, intervals)]
+        for m in range(M):
+            state = [stencil(cf, 0, u) for u in state]
+        for u, k in zip(state, intervals):
+            rd[k] = u
+        return relaxed, state
+
+    err, entry = None, None
+    for intervals in ((0, 1, 2, 3, 4, 5, 6, 7),):
+        relaxed, resid = fine(intervals)
+        if err is None:
+            entry = jnp.where(z == 0, relaxed[0] - relaxed[0], zero)
+            err = entry
+        for k in range(0, len(intervals), 2):
+            err = coarse_two(cf, err, resid[k], resid[k + 1])[1]
+    lw[0] = err
+
     def send_main(packed, plane, slot, sem):
         pltpu.make_async_remote_copy(
             packed, lr.at[slot, pl.ds(1, 2)], s2.at[sem], r2.at[slot], at(plane, here), pl.DeviceIdType.MESH
@@ -395,35 +441,26 @@
         def pass_on(e, which, planes):
             pack_halves(e, pe.at[which])
             for plane in planes:
-                pl.semaphore_wait(ready.at[plane], 3)
                 send_three(pe.at[which], plane, 0, plane)
 
-        e = chain(entry, lambda xx: None)
-        lw[0] = e
-        pack_halves(e, pk)
+        pack_halves(lw[0], pk)
         send_sides(pk, 0, 0, 0)
         pltpu.make_async_copy(pk, lr.at[0, pl.ds(1, 2)], r2.at[0]).start()
         pl.semaphore_wait(ready.at[1], 1)
         send_window(lw.at[0], 1, 0, 1)
-        for xx in range(NX_DEV):
-            send_results(xx)
+        chain(entry, send_results)
+        square_coarse(cf, kf)
+        for plane in range(2, NZ):
+            pl.semaphore_wait(ready.at[plane], 1 if plane < 4 else 3)
         e = arrived(0)
         for j in range(1, 3):
-            e = coarse_eight(cf, e)
+            e = coarse_eight(kf, e)
             window_arrived(j - 1)
             e = e + ul[j - 1]
             lw[j] = e
-            pl.semaphore_wait(ready.at[j + 1], 1)
             send_window(lw.at[j], j + 1, 0, j + 1)
-        pass_on(e, 0, (6, 5, 4))
-        pass_on(coarse_eight(cf, e), 1, (7,))
-
-    @pl.when(z > 0)
-    def _():
-        local_last = zero
-        for k in range(0, 8, 2):
-            local_last = coarse_two(cf, local_last, rd[k], rd[k + 1])[1]
-        lw[0] = local_last
+        pass_on(e, 0, (5, 4, 6))
+        pass_on(coarse_eight(kf, e), 1, (7,))
 
     @pl.when(jnp.logical_and(z >= 1, z <= 2))
     def _():
@@ -435,6 +472,8 @@
 
     @pl.when(z == 3)
     def _():
+        for plane in range(4, NZ):
+            pl.semaphore_wait(ready.at[plane], 1 if plane < 6 else 3)
         send_three(pk, 7, 2, 7)
 
     for plane in (7, 6, 5, 4):
@@ -448,6 +487,10 @@
         def _(plane=plane):
             send_window(lw.at[0], plane, z - (4 if plane == 7 else 3), plane)
 
+    @pl.when(z >= 4)
+    def _():
+        square_coarse(cf, kf)
+
     for slot in range(3):
 
         @pl.when((z == 4) | (z == 5) if slot == 0 else z >= 4 + slot)
@@ -472,7 +515,7 @@
     @pl.when(z >= 4)
     def _():
         e_in[...] = lax.fori_loop(
-            0, jnp.minimum(z - 3, 3), lambda j, e: coarse_eight(cf, e) + ul[j], arrived(0) + ahead_3[...]
+            0, jnp.minimum(z - 3, 3), lambda j, e: coarse_eight(kf, e) + ul[j], arrived(0) + ahead_3[...]
         )
 
     @pl.when(z > 0)
@@ -545,6 +588,7 @@
             f32((4, 64, LANES)),
             f32((64, LANES)),
             f32((20, 64, LANES)),
+            f32((13, 64, LANES)),
             f32((8, 64, LANES)),
             f32((8, 64, LANES)),
             f32((2, 16, LANES)),

time: 29.6 us -> 29.4 us (level)
  Pallas kernels: 29.5 us -> 29 us
    pallas_call x1, Pallas kernels: 27.8 us -> 27.4 us  [per_device(): pl.pallas_call(kernel, out_shape=jax.ShapeDtypeStruct((STRIPS, 8, LANES),...]
where the time goes in v7:
time: 29.4 us; the launch traced here: 29 us
  Pallas kernels  29 us (99%)
    pallas_call x1, Pallas kernels, per_device(): pl.pallas_call(kernel, out_shape=jax.ShapeDtypeStruct((STRIPS, 8, LANES),...  27.4 us
    pallas_call x1, Pallas kernels, per_device(): pl.pallas_call(place_rows, out_shape=jax.ShapeDtypeStruct((2, 8, 2048), j...  1.66 us

profile of v7, /device:TPU:161, one launch (start us, length us, event | category | flops | bytes accessed | tf_op | source)
XLA Modules:
  0.0 29.0 jit_solution(10512018015801241035)
XLA Ops:
  0.0 27.4 %cycle.1.ob = f32[32,8,128]{2,1,0:T(8,128)} custom-call(f32[8,2048]{1,0:T(8,128)} %initial.1, f32[8,2048]{1,0:T(8,128)} %source.1, f32[8,2048]{1,0:T(8,128)} %rate.1, f32[8,2048]{1,0:T(8,128)} %velx.1, f32[8,2048]{1,0:T(8,128)} %vely.1, f32[8]{0:T(128)} %strengths.1, f32[2,8,2048]{2,1,0:T(8,128)} %guess.1), custom_call_target="tpu_custom_call" | custom-call | flops 20000000 | bytes 700000 | tf_op jit(solution)/shard_map/cycle/pallas_call | solution.py:574
  27.4 1.7 %place.1 = f32[2,8,2048]{2,1,0:T(8,128)} custom-call(f32[32,8,128]{2,1,0:T(8,128)} %cycle.1.ob), custom_call_target="tpu_custom_call" | custom-call | tf_op jit(solution)/shard_map/place/pallas_call | solution.py:623

commit v8 on v7

--- a/solution.py
+++ b/solution.py
@@ -522,8 +522,6 @@
     def _():
         chain(e_in[...], send_results)
 
-    pltpu.make_async_copy(ob, ob, r3).wait()
-
     sent = sb.at[pl.ds(0, STRIPS - 1)]
     pltpu.make_async_copy(sent, sent, s1).wait()
     sent_fields = sf.at[pl.ds(0, NS - 1)]
@@ -556,6 +554,7 @@
 
     gone = ob.at[pl.ds(0, STRIPS - 1)]
     pltpu.make_async_copy(gone, gone, s3).wait()
+    pltpu.make_async_copy(ob, ob, r3).wait()
 
 
 def place_rows(ob, out):

time: 29.4 us -> 29.4 us (level)
  no operation moved by 1% of the time
where the time goes in v8:
time: 29.4 us; the launch traced here: 29 us
  Pallas kernels  29 us (99%)
    pallas_call x1, Pallas kernels, per_device(): pl.pallas_call(kernel, out_shape=jax.ShapeDtypeStruct((STRIPS, 8, LANES),...  27.3 us
    pallas_call x1, Pallas kernels, per_device(): pl.pallas_call(place_rows, out_shape=jax.ShapeDtypeStruct((2, 8, 2048), j...  1.66 us

profile of v8, /device:TPU:161, one launch (start us, length us, event | category | flops | bytes accessed | tf_op | source)
XLA Modules:
  0.0 29.0 jit_solution(15717229625302603914)
XLA Ops:
  0.0 27.3 %cycle.1.ob = f32[32,8,128]{2,1,0:T(8,128)} custom-call(f32[8,2048]{1,0:T(8,128)} %initial.1, f32[8,2048]{1,0:T(8,128)} %source.1, f32[8,2048]{1,0:T(8,128)} %rate.1, f32[8,2048]{1,0:T(8,128)} %velx.1, f32[8,2048]{1,0:T(8,128)} %vely.1, f32[8]{0:T(128)} %strengths.1, f32[2,8,2048]{2,1,0:T(8,128)} %guess.1), custom_call_target="tpu_custom_call" | custom-call | flops 20000000 | bytes 700000 | tf_op jit(solution)/shard_map/cycle/pallas_call | solution.py:573
  27.4 1.7 %place.1 = f32[2,8,2048]{2,1,0:T(8,128)} custom-call(f32[32,8,128]{2,1,0:T(8,128)} %cycle.1.ob), custom_call_target="tpu_custom_call" | custom-call | tf_op jit(solution)/shard_map/place/pallas_call | solution.py:622
